TPU v7x, 128 devices: a whole 4x4x4 slice. The times are simulated.
128 devices in a mesh: contrast: 4 (over x), pa: 2 (over core), pb: 16 (over z, y).
Axes of the slice: x: 4, y: 4, z: 4, core: 2. Of those that a mesh axis runs over, the one named last changes fastest.
Arguments:
- image: float32 [4, 2, 128, 160, 128], P('contrast', None, 'pa', 'pb'), may hold values from -9 to 9
- coil_maps: bfloat16 [4, 2, 128, 160, 128], P(None, None, 'pa', 'pb'), may hold values from -2 to 2
- kspace: bfloat16 [4, 4, 2, 128, 160, 128], P('contrast', None, None, ('pa', 'pb')), may hold values from -4 to 4
- sampling: int32 [4, 128, 160, 128], P('contrast', ('pa', 'pb')), may hold values 0 or 1
- available: int32 [4], P('contrast'), may hold values from 0 to 1, as said below
Outputs:
- image_next: float32 [4, 2, 128, 160, 128], P('contrast', None, 'pa', 'pb')
- misfit: float32 [], replicated
Inputs may be any that keep to these rules, and one draw needn't show every extreme that they name: `available`: at least one contrast is missing, and at most max(1, 1) are.
All inputs are finite; a program needn't handle non-finite values. No bound on the sum of `sampling` on one device may be relied on, other than what follows from the above.
Results may differ from a plain program's by a relative error of at most 0.0003.
Values sent between devices are 32-bit elements; how exact they have to be, the bound alone decides.
No kernel may reach another device: no remote copies, remote signals or barrier semaphores. Data moves between devices by JAX's collectives and lax.ppermute only.
A program may use at most 64 MiB of HBM per device.

v0:
```python
import functools
import math

import jax
import jax.numpy as jnp
import ml_dtypes
import numpy as np
from jax import lax
from jax.experimental import pallas as pl
from jax.experimental.pallas import tpu as pltpu
from jax.sharding import PartitionSpec as P

step_size = 1.0
threshold = 2.5
LANES = 128
VMEM_LIMIT = 40 * 1024 * 1024


def trig(length):
    index = np.arange(length)
    angles = (index[:, None] * index[None, :] % length) * (2.0 * math.pi / length)
    scale = 1.0 / math.sqrt(length)
    return np.cos(angles) * scale, np.sin(angles) * scale


def halves(table):
    high = table.astype(np.float32).astype(ml_dtypes.bfloat16)
    low = (table - high.astype(np.float64)).astype(np.float32).astype(ml_dtypes.bfloat16)
    return high, low


def left_table(table):
    high, low = halves(table)
    return np.concatenate([high, high, low], axis=1)


def right_table(table):
    high, low = halves(table)
    return np.concatenate([high, high, low], axis=0)


def split_data(value, axis):
    high = value.astype(jnp.bfloat16)
    low = (value - high.astype(jnp.float32)).astype(jnp.bfloat16)
    return jnp.concatenate([high, low, high], axis=axis)


def dot(left, right, dims):
    return lax.dot_general(left, right, (dims, ((), ())), preferred_element_type=jnp.float32)


def z_forward_table(depth):
    c, s = trig(depth)
    re_row = np.concatenate([c, s], axis=1)
    im_row = np.concatenate([-s, c], axis=1)
    return left_table(np.stack([re_row, im_row], axis=1).reshape(2 * depth, 2 * depth))


def z_inverse_table(depth):
    c, s = trig(depth)
    re_row = np.concatenate([c, s], axis=1)
    im_row = np.concatenate([-s, c], axis=1)
    return right_table(np.stack([re_row, im_row], axis=1).reshape(2 * depth, 2 * depth))


def x_table(width, sign):
    c, s = trig(width)
    s = sign * s
    return right_table(np.concatenate([np.concatenate([c, s], 1), np.concatenate([-s, c], 1)], 0))


def y_order(groups, rows):
    y = np.arange(groups * rows).reshape(groups, rows // 2, 2)
    return y.transpose(2, 0, 1).reshape(-1)


def y_forward_table(width, order):
    c, s = trig(width)
    return left_table(np.concatenate([c[:, order], s[:, order]], axis=0))


def y_inverse_table(width, order):
    c, s = trig(width)
    return left_table(np.concatenate([c[order], s[order]], axis=0))


def z_forward_kernel(image_ref, maps_ref, table_ref, out_ref):
    rows = image_ref.shape[1] * image_ref.shape[2]
    depth = image_ref.shape[3]
    image_re = image_ref[0].reshape(rows, depth)
    image_im = image_ref[1].reshape(rows, depth)
    maps_re = maps_ref[0, 0].reshape(rows, depth).astype(jnp.float32)
    maps_im = maps_ref[0, 1].reshape(rows, depth).astype(jnp.float32)
    product = jnp.concatenate(
        [maps_re * image_re - maps_im * image_im, maps_re * image_im + maps_im * image_re], axis=1
    )
    result = dot(table_ref[...], split_data(product, 1), ((1,), (1,)))
    parts = out_ref.shape[0]
    for tile in range(out_ref.shape[2]):
        out_ref[:, 0, tile] = result[:, tile * LANES : (tile + 1) * LANES].reshape(
            parts, out_ref.shape[3], LANES
        )


def plane_kernel(
    present_ref, in_ref, kspace_ref, sampling_ref, xf_ref, yf_ref, yi_ref, xi_ref, out_ref, misfit_ref
):
    parts, _, tiles, sub, _ = in_ref.shape
    planes = sub // 2
    rows = parts // 2 * tiles
    width_y = kspace_ref.shape[3]
    present = present_ref[0].astype(jnp.float32)
    flat_in = in_ref.reshape(parts * tiles * sub, LANES)
    flat_out = out_ref.reshape(parts * tiles * sub, LANES)
    half = LANES // 2
    low_lanes = lax.broadcasted_iota(jnp.int32, (rows, LANES), 1) < half

    def interleave(first, second):
        even = jnp.where(low_lanes, first, pltpu.roll(second, half, 1))
        odd = jnp.where(low_lanes, pltpu.roll(first, half, 1), second)
        return even, odd

    gathered = []
    for plane in range(planes):
        sides = []
        for part in range(2):
            at = 2 * plane + part
            first = flat_in[pl.ds(at, rows, stride=sub), :]
            second = flat_in[pl.ds(rows * sub + at, rows, stride=sub), :]
            sides.append(jnp.concatenate(interleave(first, second), axis=0))
        gathered.append(jnp.concatenate(sides, axis=1))
    after_x = dot(split_data(jnp.concatenate(gathered, axis=0), 1), xf_ref[...], ((1,), (0,)))
    total = jnp.zeros((8, LANES), jnp.float32)
    back = []
    for plane in range(planes):
        data = after_x[plane * width_y : (plane + 1) * width_y]
        both = dot(yf_ref[...], split_data(data, 0), ((1,), (0,)))
        spectrum_re = both[:width_y, :LANES] + both[width_y:, LANES:]
        spectrum_im = both[:width_y, LANES:] - both[width_y:, :LANES]
        weight = sampling_ref[plane].astype(jnp.float32) * present
        residual_re = weight * (spectrum_re - kspace_ref[0, 0, plane].astype(jnp.float32))
        residual_im = weight * (spectrum_im - kspace_ref[0, 1, plane].astype(jnp.float32))
        square = residual_re * residual_re + residual_im * residual_im
        total = total + jnp.sum(square.reshape(width_y // 8, 8, LANES), axis=0)
        residual = jnp.concatenate([residual_re, residual_im], axis=1)
        both = dot(yi_ref[...], split_data(residual, 0), ((1,), (0,)))
        back_re = both[:width_y, :LANES] - both[width_y:, LANES:]
        back_im = both[:width_y, LANES:] + both[width_y:, :LANES]
        back.append(jnp.concatenate([back_re, back_im], axis=1))
    returned = dot(split_data(jnp.concatenate(back, axis=0), 1), xi_ref[...], ((1,), (0,)))
    for plane in range(planes):
        for part in range(2):
            at = 2 * plane + part
            block = returned[
                plane * width_y : (plane + 1) * width_y, part * LANES : (part + 1) * LANES
            ]
            first, second = interleave(block[:rows], block[rows:])
            flat_out[pl.ds(at, rows, stride=sub), :] = first
            flat_out[pl.ds(rows * sub + at, rows, stride=sub), :] = second

    @pl.when(pl.program_id(0) == 0)
    def _():
        misfit_ref[...] = total

    @pl.when(pl.program_id(0) > 0)
    def _():
        misfit_ref[...] += total


def z_inverse_kernel(
    present_ref, in_ref, maps_ref, image_ref, table_ref, moved_ref, energy_a_ref, energy_b_ref
):
    parts, coils, _, sub, _ = in_ref.shape
    depth = image_ref.shape[3]
    present = present_ref[0].astype(jnp.float32)
    grad_re = jnp.zeros((LANES, depth), jnp.float32)
    grad_im = jnp.zeros((LANES, depth), jnp.float32)
    for coil in range(coils):
        data = in_ref[:, coil, 0].reshape(parts * sub, LANES)
        result = dot(split_data(data, 0), table_ref[...], ((0,), (0,)))
        back_re = result[:, :depth]
        back_im = result[:, depth:]
        maps_re = maps_ref[coil, 0].reshape(LANES, depth).astype(jnp.float32)
        maps_im = maps_ref[coil, 1].reshape(LANES, depth).astype(jnp.float32)
        grad_re = grad_re + (maps_re * back_re + maps_im * back_im)
        grad_im = grad_im + (maps_re * back_im - maps_im * back_re)
    shape = image_ref.shape[1:]
    moved_re = image_ref[0] - step_size * grad_re.reshape(shape)
    moved_im = image_ref[1] - step_size * grad_im.reshape(shape)
    moved_ref[0] = moved_re
    moved_ref[1] = moved_im
    energy = present * (moved_re * moved_re + moved_im * moved_im)
    cut = shape[1] // 2
    energy_a_ref[...] = energy[:, :cut]
    energy_b_ref[...] = energy[:, cut:]


def whole(array):
    zeros = (0,) * array.ndim
    return pl.BlockSpec(array.shape, lambda *_: zeros)


def params():
    return pltpu.CompilerParams(
        dimension_semantics=("arbitrary",), vmem_limit_bytes=VMEM_LIMIT
    )


def butterfly(value, axis):
    size = lax.axis_size(axis)
    span = 1
    while span < size:
        value = value + lax.ppermute(value, axis, [(i, i ^ span) for i in range(size)])
        span *= 2
    return value


def per_device(image, coil_maps, kspace, sampling, available):
    pa = lax.axis_size("pa")
    pb = lax.axis_size("pb")
    pixels = jnp.transpose(image[0], (0, 2, 1, 3))
    maps = jnp.transpose(coil_maps, (0, 1, 3, 2, 4))
    samples = kspace[0]
    mask = sampling[0]
    _, y_rows, x_rows, depth = pixels.shape
    coils = maps.shape[0]
    parts = pa * pb
    sub = 2 * depth // parts
    tiles = y_rows * x_rows // LANES
    width_x = x_rows * pa
    width_y = y_rows * pb
    order = y_order(pb, y_rows)
    zf = jnp.asarray(z_forward_table(depth))
    zi = jnp.asarray(z_inverse_table(depth))
    xf = jnp.asarray(x_table(width_x, -1.0))
    xi = jnp.asarray(x_table(width_x, 1.0))
    yf = jnp.asarray(y_forward_table(width_y, order))
    yi = jnp.asarray(y_inverse_table(width_y, order))
    buffer = jax.ShapeDtypeStruct((parts, coils, tiles, sub, LANES), jnp.float32)
    coil_block = pl.BlockSpec((parts, 1, tiles, sub, LANES), lambda j: (0, j, 0, 0, 0))
    scalar = pl.BlockSpec(memory_space=pltpu.SMEM)

    forward = pl.pallas_call(
        z_forward_kernel,
        grid=(coils,),
        out_shape=buffer,
        in_specs=[
            whole(pixels),
            pl.BlockSpec((1, 2, y_rows, x_rows, depth), lambda j: (j, 0, 0, 0, 0)),
            whole(zf),
        ],
        out_specs=coil_block,
        compiler_params=params(),
    )(pixels, maps, zf)
    received = lax.all_to_all(forward, ("pa", "pb"), split_axis=0, concat_axis=0, tiled=True)
    residual, misfit_tile = pl.pallas_call(
        plane_kernel,
        grid=(coils,),
        out_shape=(buffer, jax.ShapeDtypeStruct((8, LANES), jnp.float32)),
        in_specs=[
            scalar,
            coil_block,
            pl.BlockSpec((1,) + samples.shape[1:], lambda j: (j, 0, 0, 0, 0)),
            whole(mask),
            whole(xf),
            whole(yf),
            whole(yi),
            whole(xi),
        ],
        out_specs=(coil_block, pl.BlockSpec((8, LANES), lambda j: (0, 0))),
        compiler_params=params(),
    )(available, received, samples, mask, xf, yf, yi, xi)
    returned = lax.all_to_all(residual, ("pa", "pb"), split_axis=0, concat_axis=0, tiled=True)
    for axis in ("pb", "pa", "contrast"):
        misfit_tile = butterfly(misfit_tile, axis)
    misfit_sum = jnp.sum(misfit_tile)

    pair = LANES // x_rows
    half_energy = jax.ShapeDtypeStruct((y_rows, x_rows // 2, depth), jnp.float32)
    half_block = pl.BlockSpec((pair, x_rows // 2, depth), lambda t: (t, 0, 0))
    image_block = pl.BlockSpec((2, pair, x_rows, depth), lambda t: (0, t, 0, 0))
    moved, energy_a, energy_b = pl.pallas_call(
        z_inverse_kernel,
        grid=(tiles,),
        out_shape=(jax.ShapeDtypeStruct(pixels.shape, jnp.float32), half_energy, half_energy),
        in_specs=[
            scalar,
            pl.BlockSpec((parts, coils, 1, sub, LANES), lambda t: (0, 0, t, 0, 0)),
            pl.BlockSpec((coils, 2, pair, x_rows, depth), lambda t: (0, 0, t, 0, 0)),
            image_block,
            whole(zi),
        ],
        out_specs=(image_block, half_block, half_block),
        compiler_params=params(),
    )(available, returned, maps, pixels, zi)

    def swap(value, shift):
        size = lax.axis_size("contrast")
        pairs = []
        for low in range(shift, size + shift, 2):
            first, second = low % size, (low + 1) % size
            pairs += [(first, second), (second, first)]
        return value + lax.ppermute(value, "contrast", pairs)

    energy_a, energy_b = swap(energy_a, 0), swap(energy_b, 1)
    energy_a, energy_b = swap(energy_a, 1), swap(energy_b, 0)
    norm_value = jnp.sqrt(jnp.concatenate([energy_a, energy_b], axis=1))
    present = available[0].astype(jnp.float32)
    factor = jnp.maximum(norm_value - threshold, 0.0) / jnp.maximum(norm_value, threshold)
    shrink = present * factor
    result = jnp.transpose(moved * shrink[None], (0, 2, 1, 3))[None]
    count_all = (
        lax.axis_size("contrast") * image.shape[0] * coils * width_x * width_y * depth
    )
    return (result, misfit_sum / (2.0 * count_all))


def solution(mesh):
    return jax.shard_map(
        per_device,
        mesh=mesh,
        in_specs=(
            P("contrast", None, "pa", "pb", None),
            P(None, None, "pa", "pb", None),
            P("contrast", None, None, ("pa", "pb"), None, None),
            P("contrast", ("pa", "pb"), None, None),
            P("contrast"),
        ),
        out_specs=(P("contrast", None, "pa", "pb", None), P()),
        check_vma=False,
    )
```

profile of v0, /device:TPU:0, one launch (start us, length us, event | category | flops | bytes accessed | tf_op | source)
XLA Modules:
  0.0 146.3 jit_solution(15929414896197688097)
XLA Ops:
  0.6 0.0 copy-start.1
  0.6 1.3 copy-done.1
  1.9 0.0 copy-start.3
  2.0 1.1 copy-done.3
  3.0 0.0 copy-start.9
  3.0 1.0 copy-done.9
  4.0 2.2 %shard_map.122 = f32[32,4,5,8,128]{4,3,2,1,0:T(8,128)S(1)} custom-call(f32[2,10,64,128]{3,2,1,0:T(8,128)S(1)} %bitcast.13, bf16[4,2,10,64,128]{4,3,2,1,0:T(8,128)(2,1)S(1)} %bitcast.11, bf16[256,768]{1,0:T(8,128)(2,1)S(1)} %copy-done.9), custom_call_target="tpu_custom_call" | custom-call | tf_op jit(solution)/shard_map/pallas_call | solution.py:243
  6.2 0.0 copy-start
  6.2 1.5 %copy-done = f32[32,4,5,8,128]{4,3,2,1,0:T(8,128)} copy-done((f32[32,4,5,8,128]{4,3,2,1,0:T(8,128)}, f32[32,4,5,8,128]{4,3,2,1,0:T(8,128)S(1)}, u32[]{:S(2)}) %copy-start) | copy-done | bytes 2621464
  7.7 0.0 copy-start.7
  7.7 0.0 copy-start.8
  7.7 8.6 %all-to-all-start = ((f32[32,4,5,8,128]{4,3,2,1,0:T(8,128)}), f32[32,4,5,8,128]{4,3,2,1,0:T(8,128)S(1)}, u32[]{:S(2)}, u32[]{:S(2)}) async-start(f32[32,4,5,8,128]{4,3,2,1,0:T(8,128)} %copy-done), calls=%async_computation | async-start | bytes 5242880 | tf_op jit(solution)/shard_map/all_to_all | solution.py:255
  16.9 34.7 %all-to-all-done.in_ref = f32[32,4,5,8,128]{4,3,2,1,0:T(8,128)S(1)} async-done(((f32[32,4,5,8,128]{4,3,2,1,0:T(8,128)}), f32[32,4,5,8,128]{4,3,2,1,0:T(8,128)S(1)}, u32[]{:S(2)}, u32[]{:S(2)}) %all-to-all-start) | async-done | bytes 2621472 | tf_op jit(solution)/shard_map/all_to_all | solution.py:255
  51.6 0.0 copy-done.7
  51.6 0.0 copy-done.8
  51.6 0.0 copy-start.5
  51.6 1.3 copy-done.5
  53.0 0.0 copy-start.10
  53.0 1.0 copy-done.10
  53.9 0.0 copy-start.11
  53.9 1.0 copy-done.11
  54.9 0.0 copy-start.12
  54.9 1.0 copy-done.12
  55.9 9.9 %shard_map.123 = (f32[32,4,5,8,128]{4,3,2,1,0:T(8,128)S(1)}, f32[8,128]{1,0:T(8,128)S(1)}) custom-call(s32[1]{0:T(128)S(6)} %copy.13.present_ref, f32[32,4,5,8,128]{4,3,2,1,0:T(8,128)S(1)} %all-to-all-done.in_ref, bf16[4,2,4,160,128]{4,3,2,1,0:T(8,128)(2,1)S(1)} %bitcast.15, s32[4,160,128]{2,1,0:T(8,128)S(1)} %bitcast.16, bf16[768,256]{1,0:T(8,128)(2,1)S(1)} %copy-done.7, ...), custom_call_target="tpu_custom_call" | custom-call | tf_op jit(solution)/shard_map/pallas_call | solution.py:256
  65.8 0.0 copy-start.2
  65.8 0.0 copy-start.4
  65.8 0.0 copy-start.6
  65.8 38.1 %all_to_all.10.in_ref = f32[32,4,5,8,128]{4,3,2,1,0:T(8,128)S(1)} all-to-all(f32[32,4,5,8,128]{4,3,2,1,0:T(8,128)S(1)} %get-tuple-element.7), channel_id=1, replica_groups=mesh['contrast'=4,'pa'=2,'pb'=16] {'pa','pb'}, dimensions={0} | all-to-all | bytes 5242880 | tf_op jit(solution)/shard_map/all_to_all | solution.py:273
  104.0 0.0 copy-done.2
  104.0 0.0 copy-done.4
  104.0 0.0 copy-done.6
  104.0 2.6 %shard_map.124 = (f32[2,10,64,128]{3,2,1,0:T(8,128)S(1)}, f32[10,32,128]{2,1,0:T(8,128)S(1)}, f32[10,32,128]{2,1,0:T(8,128)S(1)}) custom-call(s32[1]{0:T(128)S(6)} %copy.13.present_ref, f32[32,4,5,8,128]{4,3,2,1,0:T(8,128)S(1)} %all_to_all.10.in_ref, bf16[4,2,10,64,128]{4,3,2,1,0:T(8,128)(2,1)S(1)} %bitcast.12, f32[2,10,64,128]{3,2,1,0:T(8,128)S(1)} %bitcast.14, ...), custom_call_target="tpu_custom_call" | custom-call | tf_op jit(solution)/shard_map/pallas_call | solution.py:282
  106.6 1.6 %collective-permute-start = (f32[10,32,128]{2,1,0:T(8,128)S(1)}, f32[10,32,128]{2,1,0:T(8,128)S(1)}, u32[]{:S(2)}, u32[]{:S(2)}) collective-permute-start(f32[10,32,128]{2,1,0:T(8,128)S(1)} %get-tuple-element.9), channel_id=1, source_target_pairs={{0,32},{32,0},{64,96},{96,64},{1,33},{33,1},{65,97},{97,65},{2,34}... | collective-permute-start | bytes 491528 | tf_op jit(solution)/shard_map/ppermute | solution.py:303
  108.2 2.1 %collective-permute-start.2 = (f32[10,32,128]{2,1,0:T(8,128)S(1)}, f32[10,32,128]{2,1,0:T(8,128)S(1)}, u32[]{:S(2)}, u32[]{:S(2)}) collective-permute-start(f32[10,32,128]{2,1,0:T(8,128)S(1)} %get-tuple-element.10), channel_id=1, source_target_pairs={{32,64},{64,32},{96,0},{0,96},{33,65},{65,33},{97,1},{1,97},{34,66... | collective-permute-start | bytes 491528 | tf_op jit(solution)/shard_map/ppermute | solution.py:303
  110.3 1.9 %collective-permute-done = f32[10,32,128]{2,1,0:T(8,128)S(1)} collective-permute-done((f32[10,32,128]{2,1,0:T(8,128)S(1)}, f32[10,32,128]{2,1,0:T(8,128)S(1)}, u32[]{:S(2)}, u32[]{:S(2)}) %collective-permute-start) | collective-permute-done | bytes 163872 | tf_op jit(solution)/shard_map/ppermute | solution.py:303
  112.2 2.8 %collective-permute-start.1 = (f32[10,32,128]{2,1,0:T(8,128)S(1)}, f32[10,32,128]{2,1,0:T(8,128)S(1)}, u32[]{:S(2)}, u32[]{:S(2)}) collective-permute-start(f32[10,32,128]{2,1,0:T(8,128)S(1)} %add.38), channel_id=1, source_target_pairs={{32,64},{64,32},{96,0},{0,96},{33,65},{65,33},{97,1},{1,97},{34,66... | collective-permute-start | bytes 491528 | tf_op jit(solution)/shard_map/ppermute | solution.py:303
  115.1 0.0 collective-permute-done.2
  115.1 0.3 collective-permute-start.3
  115.4 0.1 collective-permute-start.4
  115.5 3.5 %collective-permute-done.4 = f32[8,128]{1,0:T(8,128)S(1)} collective-permute-done((f32[8,128]{1,0:T(8,128)S(1)}, f32[8,128]{1,0:T(8,128)S(1)}, u32[]{:S(2)}, u32[]{:S(2)}) %collective-permute-start.4) | collective-permute-done | bytes 4128 | tf_op jit(solution)/shard_map/ppermute | solution.py:213
  119.0 1.8 %collective-permute-start.5 = (f32[8,128]{1,0:T(8,128)S(1)}, f32[8,128]{1,0:T(8,128)S(1)}, u32[]{:S(2)}, u32[]{:S(2)}) collective-permute-start(f32[8,128]{1,0:T(8,128)S(1)} %add.42), channel_id=1, source_target_pairs={{0,2},{1,3},{2,0},{3,1},{4,6},{5,7},{6,4},{7,5},{8,10},{9,11},{10,... | collective-permute-start | bytes 12296 | tf_op jit(solution)/shard_map/ppermute | solution.py:213
  120.8 3.3 %collective-permute-done.5 = f32[8,128]{1,0:T(8,128)S(1)} collective-permute-done((f32[8,128]{1,0:T(8,128)S(1)}, f32[8,128]{1,0:T(8,128)S(1)}, u32[]{:S(2)}, u32[]{:S(2)}) %collective-permute-start.5) | collective-permute-done | bytes 4128 | tf_op jit(solution)/shard_map/ppermute | solution.py:213
  124.1 0.9 collective-permute-start.6
  125.1 2.7 %collective-permute-done.6 = f32[8,128]{1,0:T(8,128)S(1)} collective-permute-done((f32[8,128]{1,0:T(8,128)S(1)}, f32[8,128]{1,0:T(8,128)S(1)}, u32[]{:S(2)}, u32[]{:S(2)}) %collective-permute-start.6) | collective-permute-done | bytes 4128 | tf_op jit(solution)/shard_map/ppermute | solution.py:213
  127.7 1.7 %collective-permute-start.7 = (f32[8,128]{1,0:T(8,128)S(1)}, f32[8,128]{1,0:T(8,128)S(1)}, u32[]{:S(2)}, u32[]{:S(2)}) collective-permute-start(f32[8,128]{1,0:T(8,128)S(1)} %add.44), channel_id=1, source_target_pairs={{0,8},{1,9},{2,10},{3,11},{4,12},{5,13},{6,14},{7,15},{8,0},{9,1},... | collective-permute-start | bytes 12296 | tf_op jit(solution)/shard_map/ppermute | solution.py:213
  129.4 3.4 %collective-permute-done.7 = f32[8,128]{1,0:T(8,128)S(1)} collective-permute-done((f32[8,128]{1,0:T(8,128)S(1)}, f32[8,128]{1,0:T(8,128)S(1)}, u32[]{:S(2)}, u32[]{:S(2)}) %collective-permute-start.7) | collective-permute-done | bytes 4128 | tf_op jit(solution)/shard_map/ppermute | solution.py:213
  132.9 0.0 collective-permute-start.8
  132.9 1.2 collective-permute-done.8
  134.0 1.8 %collective-permute-start.9 = (f32[8,128]{1,0:T(8,128)S(1)}, f32[8,128]{1,0:T(8,128)S(1)}, u32[]{:S(2)}, u32[]{:S(2)}) collective-permute-start(f32[8,128]{1,0:T(8,128)S(1)} %add.46), channel_id=1, source_target_pairs={{0,32},{32,0},{64,96},{96,64},{1,33},{33,1},{65,97},{97,65},{2,34}... | collective-permute-start | bytes 12296 | tf_op jit(solution)/shard_map/ppermute | solution.py:213
  135.8 1.8 %collective-permute-done.9 = f32[8,128]{1,0:T(8,128)S(1)} collective-permute-done((f32[8,128]{1,0:T(8,128)S(1)}, f32[8,128]{1,0:T(8,128)S(1)}, u32[]{:S(2)}, u32[]{:S(2)}) %collective-permute-start.9) | collective-permute-done | bytes 4128 | tf_op jit(solution)/shard_map/ppermute | solution.py:213
  137.6 3.0 %collective-permute-start.10 = (f32[8,128]{1,0:T(8,128)S(1)}, f32[8,128]{1,0:T(8,128)S(1)}, u32[]{:S(2)}, u32[]{:S(2)}) collective-permute-start(f32[8,128]{1,0:T(8,128)S(1)} %add.47), channel_id=1, source_target_pairs={{0,64},{32,96},{64,0},{96,32},{1,65},{33,97},{65,1},{97,33},{2,66}... | collective-permute-start | bytes 12296 | tf_op jit(solution)/shard_map/ppermute | solution.py:213
  140.6 2.1 %collective-permute-done.10 = f32[8,128]{1,0:T(8,128)S(1)} collective-permute-done((f32[8,128]{1,0:T(8,128)S(1)}, f32[8,128]{1,0:T(8,128)S(1)}, u32[]{:S(2)}, u32[]{:S(2)}) %collective-permute-start.10) | collective-permute-done | bytes 4128 | tf_op jit(solution)/shard_map/ppermute | solution.py:213
  142.7 0.6 add_reduce_fusion
  144.0 0.0 collective-permute-done.1
  144.0 0.0 collective-permute-done.3
  144.1 0.2 divide_multiply_fusion
  144.2 0.9 multiply_bitcast_fusion
  (10 shorter events, 0.1 us)
Async XLA Ops:
  0.6 1.3 copy-start.1
  1.9 1.1 copy-start.3
  3.0 1.0 copy-start.9
  6.2 1.5 %copy-start = (f32[32,4,5,8,128]{4,3,2,1,0:T(8,128)}, f32[32,4,5,8,128]{4,3,2,1,0:T(8,128)S(1)}, u32[]{:S(2)}) copy-start(f32[32,4,5,8,128]{4,3,2,1,0:T(8,128)S(1)} %shard_map.122) | copy-start | bytes 7864324
  7.7 43.9 %copy-start.7 = (bf16[768,256]{1,0:T(8,128)(2,1)S(1)}, bf16[768,256]{1,0:T(8,128)(2,1)}, u32[]{:S(2)}) copy-start(bf16[768,256]{1,0:T(8,128)(2,1)} %constant.24.clone.xf_ref) | copy-start | bytes 1179652
  7.7 43.9 %copy-start.8 = (bf16[768,256]{1,0:T(8,128)(2,1)S(1)}, bf16[768,256]{1,0:T(8,128)(2,1)}, u32[]{:S(2)}) copy-start(bf16[768,256]{1,0:T(8,128)(2,1)} %constant.25.clone.xi_ref) | copy-start | bytes 1179652
  7.7 43.9 %all-to-all-start = ((f32[32,4,5,8,128]{4,3,2,1,0:T(8,128)}), f32[32,4,5,8,128]{4,3,2,1,0:T(8,128)S(1)}, u32[]{:S(2)}, u32[]{:S(2)}) async-start(f32[32,4,5,8,128]{4,3,2,1,0:T(8,128)} %copy-done), calls=%async_computation | async-start | bytes 5242880 | tf_op jit(solution)/shard_map/all_to_all | solution.py:255
  51.6 1.3 copy-start.5
  53.0 1.0 copy-start.10
  53.9 1.0 copy-start.11
  54.9 1.0 copy-start.12
  65.8 38.2 %copy-start.2 = (bf16[4,2,64,10,128]{4,2,3,1,0:T(8,128)(2,1)S(1)}, bf16[4,2,64,10,128]{4,2,3,1,0:T(8,128)(2,1)}, u32[]{:S(2)}) copy-start(bf16[4,2,64,10,128]{4,2,3,1,0:T(8,128)(2,1)} %param.12) | copy-start | bytes 3932164
  65.8 38.2 %copy-start.4 = (f32[1,2,64,10,128]{4,2,3,1,0:T(8,128)S(1)}, f32[1,2,64,10,128]{4,2,3,1,0:T(8,128)}, u32[]{:S(2)}) copy-start(f32[1,2,64,10,128]{4,2,3,1,0:T(8,128)} %param.11) | copy-start | bytes 1966084
  65.8 38.1 %copy-start.6 = (bf16[768,256]{1,0:T(8,128)(2,1)S(1)}, bf16[768,256]{1,0:T(8,128)(2,1)}, u32[]{:S(2)}) copy-start(bf16[768,256]{1,0:T(8,128)(2,1)} %constant.23.clone.table_ref) | copy-start | bytes 1179652
  106.6 5.6 %collective-permute-start = (f32[10,32,128]{2,1,0:T(8,128)S(1)}, f32[10,32,128]{2,1,0:T(8,128)S(1)}, u32[]{:S(2)}, u32[]{:S(2)}) collective-permute-start(f32[10,32,128]{2,1,0:T(8,128)S(1)} %get-tuple-element.9), channel_id=1, source_target_pairs={{0,32},{32,0},{64,96},{96,64},{1,33},{33,1},{65,97},{97,65},{2,34}... | collective-permute-start | bytes 491528 | tf_op jit(solution)/shard_map/ppermute | solution.py:303
  108.2 6.9 %collective-permute-start.2 = (f32[10,32,128]{2,1,0:T(8,128)S(1)}, f32[10,32,128]{2,1,0:T(8,128)S(1)}, u32[]{:S(2)}, u32[]{:S(2)}) collective-permute-start(f32[10,32,128]{2,1,0:T(8,128)S(1)} %get-tuple-element.10), channel_id=1, source_target_pairs={{32,64},{64,32},{96,0},{0,96},{33,65},{65,33},{97,1},{1,97},{34,66... | collective-permute-start | bytes 491528 | tf_op jit(solution)/shard_map/ppermute | solution.py:303
  112.2 31.8 %collective-permute-start.1 = (f32[10,32,128]{2,1,0:T(8,128)S(1)}, f32[10,32,128]{2,1,0:T(8,128)S(1)}, u32[]{:S(2)}, u32[]{:S(2)}) collective-permute-start(f32[10,32,128]{2,1,0:T(8,128)S(1)} %add.38), channel_id=1, source_target_pairs={{32,64},{64,32},{96,0},{0,96},{33,65},{65,33},{97,1},{1,97},{34,66... | collective-permute-start | bytes 491528 | tf_op jit(solution)/shard_map/ppermute | solution.py:303
  115.1 29.0 %collective-permute-start.3 = (f32[10,32,128]{2,1,0:T(8,128)S(1)}, f32[10,32,128]{2,1,0:T(8,128)S(1)}, u32[]{:S(2)}, u32[]{:S(2)}) collective-permute-start(f32[10,32,128]{2,1,0:T(8,128)S(1)} %add.40), channel_id=1, source_target_pairs={{0,32},{32,0},{64,96},{96,64},{1,33},{33,1},{65,97},{97,65},{2,34}... | collective-permute-start | bytes 491528 | tf_op jit(solution)/shard_map/ppermute | solution.py:303
  115.4 3.6 %collective-permute-start.4 = (f32[8,128]{1,0:T(8,128)S(1)}, f32[8,128]{1,0:T(8,128)S(1)}, u32[]{:S(2)}, u32[]{:S(2)}) collective-permute-start(f32[8,128]{1,0:T(8,128)S(1)} %get-tuple-element.11), channel_id=1, source_target_pairs={{0,1},{1,0},{2,3},{3,2},{4,5},{5,4},{6,7},{7,6},{8,9},{9,8},{10,11... | collective-permute-start | bytes 12296 | tf_op jit(solution)/shard_map/ppermute | solution.py:213
  119.0 5.1 %collective-permute-start.5 = (f32[8,128]{1,0:T(8,128)S(1)}, f32[8,128]{1,0:T(8,128)S(1)}, u32[]{:S(2)}, u32[]{:S(2)}) collective-permute-start(f32[8,128]{1,0:T(8,128)S(1)} %add.42), channel_id=1, source_target_pairs={{0,2},{1,3},{2,0},{3,1},{4,6},{5,7},{6,4},{7,5},{8,10},{9,11},{10,... | collective-permute-start | bytes 12296 | tf_op jit(solution)/shard_map/ppermute | solution.py:213
  124.1 3.6 %collective-permute-start.6 = (f32[8,128]{1,0:T(8,128)S(1)}, f32[8,128]{1,0:T(8,128)S(1)}, u32[]{:S(2)}, u32[]{:S(2)}) collective-permute-start(f32[8,128]{1,0:T(8,128)S(1)} %add.43), channel_id=1, source_target_pairs={{0,4},{1,5},{2,6},{3,7},{4,0},{5,1},{6,2},{7,3},{8,12},{9,13},{10,... | collective-permute-start | bytes 12296 | tf_op jit(solution)/shard_map/ppermute | solution.py:213
  127.7 5.1 %collective-permute-start.7 = (f32[8,128]{1,0:T(8,128)S(1)}, f32[8,128]{1,0:T(8,128)S(1)}, u32[]{:S(2)}, u32[]{:S(2)}) collective-permute-start(f32[8,128]{1,0:T(8,128)S(1)} %add.44), channel_id=1, source_target_pairs={{0,8},{1,9},{2,10},{3,11},{4,12},{5,13},{6,14},{7,15},{8,0},{9,1},... | collective-permute-start | bytes 12296 | tf_op jit(solution)/shard_map/ppermute | solution.py:213
  132.9 1.2 collective-permute-start.8
  134.0 3.6 %collective-permute-start.9 = (f32[8,128]{1,0:T(8,128)S(1)}, f32[8,128]{1,0:T(8,128)S(1)}, u32[]{:S(2)}, u32[]{:S(2)}) collective-permute-start(f32[8,128]{1,0:T(8,128)S(1)} %add.46), channel_id=1, source_target_pairs={{0,32},{32,0},{64,96},{96,64},{1,33},{33,1},{65,97},{97,65},{2,34}... | collective-permute-start | bytes 12296 | tf_op jit(solution)/shard_map/ppermute | solution.py:213
  137.6 5.1 %collective-permute-start.10 = (f32[8,128]{1,0:T(8,128)S(1)}, f32[8,128]{1,0:T(8,128)S(1)}, u32[]{:S(2)}, u32[]{:S(2)}) collective-permute-start(f32[8,128]{1,0:T(8,128)S(1)} %add.47), channel_id=1, source_target_pairs={{0,64},{32,96},{64,0},{96,32},{1,65},{33,97},{65,1},{97,33},{2,66}... | collective-permute-start | bytes 12296 | tf_op jit(solution)/shard_map/ppermute | solution.py:213
where the time goes:
time: 147 us; the launch traced here: 146 us
  waiting for transfers between devices  54.7 us (37%)
  blocking collectives  38.1 us (26%)
  starting transfers between devices  24.6 us (17%)
  Pallas kernels  14.7 us (10%)
  local copies, waits for them, and re-layouts  9.15 us (6%)
  between operations  3.2 us (2%)
  other arithmetic  1.77 us (1%)
    all_to_all x1, blocking collectives, per_device(): lax.all_to_all(residual, ('pa', 'pb'), split_axis=0, concat_axis=0, tiled...  38.1 us
    all_to_all x1, waiting for transfers between devices, per_device(): lax.all_to_all(forward, ('pa', 'pb'), split_axis=0, concat_axis=0, tiled=...  34.7 us
    ppermute x7, waiting for transfers between devices, butterfly(): lax.ppermute(value, axis, [(i, i ^ span) for i in range(size)])  18.1 us
    pallas_call x1, Pallas kernels, per_device(): pl.pallas_call(plane_kernel, grid=(coils,), out_shape=(buffer, jax.ShapeD...  9.9 us
    ppermute x7, starting transfers between devices, butterfly(): lax.ppermute(value, axis, [(i, i ^ span) for i in range(size)])  9.24 us
    unnamed x26, local copies, waits for them, and re-layouts  9.15 us
    all_to_all x1, starting transfers between devices, per_device(): lax.all_to_all(forward, ('pa', 'pb'), split_axis=0, concat_axis=0, tiled=...  8.55 us
    ppermute x4, starting transfers between devices, swap(): return value + lax.ppermute(value, 'contrast', pairs)  6.82 us
  transfers between devices with their start and end apart: 12, of which 9 were waited for; matrix products, arithmetic and copies ran while one was open for 0% of the time, Pallas kernels for 0%

commit v1 on v0

--- a/solution.py
+++ b/solution.py
@@ -103,23 +103,47 @@
 
 
 def plane_kernel(
-    present_ref, in_ref, kspace_ref, sampling_ref, xf_ref, yf_ref, yi_ref, xi_ref, out_ref, misfit_ref
+    present_ref, in_ref, xf_ref, xi_ref, kspace_hbm, sampling_hbm, yf_hbm, yi_hbm, out_hbm,
+    kspace_ref, sampling_ref, yf_ref, yi_ref, result_ref, misfit_ref, in_sems, out_sems, last_sem,
 ):
     parts, _, tiles, sub, _ = in_ref.shape
     planes = sub // 2
     rows = parts // 2 * tiles
     width_y = kspace_ref.shape[3]
+    coil = pl.program_id(0)
+    coils = pl.num_programs(0)
+    slot = lax.rem(coil, 2)
     present = present_ref[0].astype(jnp.float32)
-    flat_in = in_ref.reshape(parts * tiles * sub, LANES)
-    flat_out = out_ref.reshape(parts * tiles * sub, LANES)
     half = LANES // 2
     low_lanes = lax.broadcasted_iota(jnp.int32, (rows, LANES), 1) < half
+    fetches = [
+        pltpu.make_async_copy(source, target, in_sems.at[n])
+        for n, (source, target) in enumerate(
+            [
+                (yf_hbm, yf_ref),
+                (sampling_hbm, sampling_ref),
+                (kspace_hbm, kspace_ref),
+                (yi_hbm, yi_ref),
+            ]
+        )
+    ]
+
+    @pl.when(coil == 0)
+    def _():
+        for fetch in fetches:
+            fetch.start()
+
+    def send(at, number):
+        return pltpu.make_async_copy(
+            result_ref.at[at], out_hbm.at[:, pl.ds(number * tiles, tiles)], out_sems.at[at]
+        )
 
     def interleave(first, second):
         even = jnp.where(low_lanes, first, pltpu.roll(second, half, 1))
         odd = jnp.where(low_lanes, pltpu.roll(first, half, 1), second)
         return even, odd
 
+    flat_in = in_ref.reshape(parts * tiles * sub, LANES)
     gathered = []
     for plane in range(planes):
         sides = []
@@ -130,6 +154,12 @@
             sides.append(jnp.concatenate(interleave(first, second), axis=0))
         gathered.append(jnp.concatenate(sides, axis=1))
     after_x = dot(split_data(jnp.concatenate(gathered, axis=0), 1), xf_ref[...], ((1,), (0,)))
+
+    @pl.when(coil == 0)
+    def _():
+        for fetch in fetches:
+            fetch.wait()
+
     total = jnp.zeros((8, LANES), jnp.float32)
     back = []
     for plane in range(planes):
@@ -138,8 +168,8 @@
         spectrum_re = both[:width_y, :LANES] + both[width_y:, LANES:]
         spectrum_im = both[:width_y, LANES:] - both[width_y:, :LANES]
         weight = sampling_ref[plane].astype(jnp.float32) * present
-        residual_re = weight * (spectrum_re - kspace_ref[0, 0, plane].astype(jnp.float32))
-        residual_im = weight * (spectrum_im - kspace_ref[0, 1, plane].astype(jnp.float32))
+        residual_re = weight * (spectrum_re - kspace_ref[coil, 0, plane].astype(jnp.float32))
+        residual_im = weight * (spectrum_im - kspace_ref[coil, 1, plane].astype(jnp.float32))
         square = residual_re * residual_re + residual_im * residual_im
         total = total + jnp.sum(square.reshape(width_y // 8, 8, LANES), axis=0)
         residual = jnp.concatenate([residual_re, residual_im], axis=1)
@@ -148,6 +178,20 @@
         back_im = both[:width_y, LANES:] + both[width_y:, :LANES]
         back.append(jnp.concatenate([back_re, back_im], axis=1))
     returned = dot(split_data(jnp.concatenate(back, axis=0), 1), xi_ref[...], ((1,), (0,)))
+
+    @pl.when(coil == 0)
+    def _():
+        misfit_ref[0, 0] = total
+
+    @pl.when(coil > 0)
+    def _():
+        misfit_ref[0, 0] += total
+
+    @pl.when(coil > 1)
+    def _():
+        send(slot, coil - 2).wait()
+
+    flat_out = result_ref.at[slot].reshape(parts * tiles * sub, LANES)
     for plane in range(planes):
         for part in range(2):
             at = 2 * plane + part
@@ -157,26 +201,31 @@
             first, second = interleave(block[:rows], block[rows:])
             flat_out[pl.ds(at, rows, stride=sub), :] = first
             flat_out[pl.ds(rows * sub + at, rows, stride=sub), :] = second
-
-    @pl.when(pl.program_id(0) == 0)
-    def _():
-        misfit_ref[...] = total
-
-    @pl.when(pl.program_id(0) > 0)
-    def _():
-        misfit_ref[...] += total
-
-
-def z_inverse_kernel(
-    present_ref, in_ref, maps_ref, image_ref, table_ref, moved_ref, energy_a_ref, energy_b_ref
-):
-    parts, coils, _, sub, _ = in_ref.shape
+    send(slot, coil).start()
+
+    @pl.when(coil == coils - 1)
+    def _():
+        misfit_ref[...] = jnp.broadcast_to(misfit_ref[0, 0][None, None], misfit_ref.shape)
+        last = pltpu.make_async_copy(
+            misfit_ref, out_hbm.at[:, pl.ds(coils * tiles, 1)], last_sem
+        )
+        last.start()
+        send(1 - slot, coil - 1).wait()
+        send(slot, coil).wait()
+        last.wait()
+
+
+def z_inverse_kernel(scale, coils, present_ref, *refs):
+    data_refs = refs[:coils]
+    misfit_ref, maps_ref, image_ref, table_ref, moved_ref, energy_ref = refs[coils:]
+    parts, _, sub, _ = misfit_ref.shape
     depth = image_ref.shape[3]
+    step = pl.program_id(0)
     present = present_ref[0].astype(jnp.float32)
     grad_re = jnp.zeros((LANES, depth), jnp.float32)
     grad_im = jnp.zeros((LANES, depth), jnp.float32)
     for coil in range(coils):
-        data = in_ref[:, coil, 0].reshape(parts * sub, LANES)
+        data = data_refs[coil][:, 0].reshape(parts * sub, LANES)
         result = dot(split_data(data, 0), table_ref[...], ((0,), (0,)))
         back_re = result[:, :depth]
         back_im = result[:, depth:]
@@ -190,9 +239,13 @@
     moved_ref[0] = moved_re
     moved_ref[1] = moved_im
     energy = present * (moved_re * moved_re + moved_im * moved_im)
-    cut = shape[1] // 2
-    energy_a_ref[...] = energy[:, :cut]
-    energy_b_ref[...] = energy[:, cut:]
+    count = LANES // 8
+    energy_ref[pl.ds(step * count, count)] = energy.reshape(count, 8, depth)
+
+    @pl.when(step == 0)
+    def _():
+        misfit = jnp.sum(misfit_ref[:, 0], axis=0)
+        energy_ref[energy_ref.shape[0] - 1] = jnp.full((8, depth), jnp.sum(misfit) * scale)
 
 
 def whole(array):
@@ -206,13 +259,8 @@
     )
 
 
-def butterfly(value, axis):
-    size = lax.axis_size(axis)
-    span = 1
-    while span < size:
-        value = value + lax.ppermute(value, axis, [(i, i ^ span) for i in range(size)])
-        span *= 2
-    return value
+def in_hbm(array):
+    return pltpu.with_memory_space_constraint(array, pltpu.HBM)
 
 
 def per_device(image, coil_maps, kspace, sampling, available):
@@ -236,7 +284,7 @@
     xi = jnp.asarray(x_table(width_x, 1.0))
     yf = jnp.asarray(y_forward_table(width_y, order))
     yi = jnp.asarray(y_inverse_table(width_y, order))
-    buffer = jax.ShapeDtypeStruct((parts, coils, tiles, sub, LANES), jnp.float32)
+    buffer = pltpu.HBM((parts, coils, tiles, sub, LANES), jnp.float32)
     coil_block = pl.BlockSpec((parts, 1, tiles, sub, LANES), lambda j: (0, j, 0, 0, 0))
     scalar = pl.BlockSpec(memory_space=pltpu.SMEM)
 
@@ -251,68 +299,76 @@
         ],
         out_specs=coil_block,
         compiler_params=params(),
-    )(pixels, maps, zf)
+    )(in_hbm(pixels), in_hbm(maps), in_hbm(zf))
     received = lax.all_to_all(forward, ("pa", "pb"), split_axis=0, concat_axis=0, tiled=True)
-    residual, misfit_tile = pl.pallas_call(
+    anywhere = pl.BlockSpec(memory_space=pl.ANY)
+    residual = pl.pallas_call(
         plane_kernel,
         grid=(coils,),
-        out_shape=(buffer, jax.ShapeDtypeStruct((8, LANES), jnp.float32)),
-        in_specs=[
-            scalar,
-            coil_block,
-            pl.BlockSpec((1,) + samples.shape[1:], lambda j: (j, 0, 0, 0, 0)),
-            whole(mask),
-            whole(xf),
-            whole(yf),
-            whole(yi),
-            whole(xi),
+        out_shape=pltpu.HBM((parts, coils * tiles + 1, sub, LANES), jnp.float32),
+        in_specs=[scalar, coil_block, whole(xf), whole(xi)] + [anywhere] * 4,
+        out_specs=anywhere,
+        scratch_shapes=[
+            pltpu.VMEM(samples.shape, samples.dtype),
+            pltpu.VMEM(mask.shape, mask.dtype),
+            pltpu.VMEM(yf.shape, yf.dtype),
+            pltpu.VMEM(yi.shape, yi.dtype),
+            pltpu.VMEM((2, parts, tiles, sub, LANES), jnp.float32),
+            pltpu.VMEM((parts, 1, sub, LANES), jnp.float32),
+            pltpu.SemaphoreType.DMA((4,)),
+            pltpu.SemaphoreType.DMA((2,)),
+            pltpu.SemaphoreType.DMA,
         ],
-        out_specs=(coil_block, pl.BlockSpec((8, LANES), lambda j: (0, 0))),
         compiler_params=params(),
-    )(available, received, samples, mask, xf, yf, yi, xi)
+    )(available, received, xf, xi, in_hbm(samples), in_hbm(mask), in_hbm(yf), in_hbm(yi))
     returned = lax.all_to_all(residual, ("pa", "pb"), split_axis=0, concat_axis=0, tiled=True)
-    for axis in ("pb", "pa", "contrast"):
-        misfit_tile = butterfly(misfit_tile, axis)
-    misfit_sum = jnp.sum(misfit_tile)
 
     pair = LANES // x_rows
-    half_energy = jax.ShapeDtypeStruct((y_rows, x_rows // 2, depth), jnp.float32)
-    half_block = pl.BlockSpec((pair, x_rows // 2, depth), lambda t: (t, 0, 0))
     image_block = pl.BlockSpec((2, pair, x_rows, depth), lambda t: (0, t, 0, 0))
-    moved, energy_a, energy_b = pl.pallas_call(
-        z_inverse_kernel,
+    contrasts = lax.axis_size("contrast") * image.shape[0]
+    scale = 1.0 / (2.0 * contrasts * coils * width_x * width_y * depth)
+    energy_tiles = y_rows * x_rows // 8
+
+    def tile_block(coil):
+        return pl.BlockSpec((parts, 1, sub, LANES), lambda t: (0, coil * tiles + t, 0, 0))
+
+    moved, energy = pl.pallas_call(
+        functools.partial(z_inverse_kernel, scale, coils),
         grid=(tiles,),
-        out_shape=(jax.ShapeDtypeStruct(pixels.shape, jnp.float32), half_energy, half_energy),
-        in_specs=[
-            scalar,
-            pl.BlockSpec((parts, coils, 1, sub, LANES), lambda t: (0, 0, t, 0, 0)),
+        out_shape=(
+            jax.ShapeDtypeStruct(pixels.shape, jnp.float32),
+            jax.ShapeDtypeStruct((energy_tiles + 1, 8, depth), jnp.float32),
+        ),
+        in_specs=[scalar]
+        + [tile_block(coil) for coil in range(coils)]
+        + [
+            pl.BlockSpec((parts, 1, sub, LANES), lambda t: (0, coils * tiles, 0, 0)),
             pl.BlockSpec((coils, 2, pair, x_rows, depth), lambda t: (0, 0, t, 0, 0)),
             image_block,
             whole(zi),
         ],
-        out_specs=(image_block, half_block, half_block),
+        out_specs=(
+            image_block,
+            pl.BlockSpec((energy_tiles + 1, 8, depth), lambda t: (0, 0, 0)),
+        ),
         compiler_params=params(),
-    )(available, returned, maps, pixels, zi)
-
-    def swap(value, shift):
-        size = lax.axis_size("contrast")
+    )(available, *[returned] * (coils + 1), maps, pixels, zi)
+
+    size = lax.axis_size("contrast")
+    for step in range(2):
         pairs = []
-        for low in range(shift, size + shift, 2):
-            first, second = low % size, (low + 1) % size
-            pairs += [(first, second), (second, first)]
-        return value + lax.ppermute(value, "contrast", pairs)
-
-    energy_a, energy_b = swap(energy_a, 0), swap(energy_b, 1)
-    energy_a, energy_b = swap(energy_a, 1), swap(energy_b, 0)
-    norm_value = jnp.sqrt(jnp.concatenate([energy_a, energy_b], axis=1))
+        for core in range(pa):
+            shift = (core + step) % 2
+            for low in range(shift, size + shift, 2):
+                first, second = low % size * pa + core, (low + 1) % size * pa + core
+                pairs += [(first, second), (second, first)]
+        energy = energy + lax.ppermute(energy, ("contrast", "pa"), pairs)
+    norm_value = jnp.sqrt(energy[:energy_tiles].reshape(y_rows, x_rows, depth))
     present = available[0].astype(jnp.float32)
     factor = jnp.maximum(norm_value - threshold, 0.0) / jnp.maximum(norm_value, threshold)
     shrink = present * factor
     result = jnp.transpose(moved * shrink[None], (0, 2, 1, 3))[None]
-    count_all = (
-        lax.axis_size("contrast") * image.shape[0] * coils * width_x * width_y * depth
-    )
-    return (result, misfit_sum / (2.0 * count_all))
+    return (result, energy[energy_tiles, 0, 0])
 
 
 def solution(mesh):

time: 147 us -> 123 us (0.84)
  starting transfers between devices: 24.6 us -> 13 us
  waiting for transfers between devices: 54.7 us -> 45.9 us
  local copies, waits for them, and re-layouts: 9.15 us -> 0.54 us
  Pallas kernels: 14.7 us -> 21 us
  blocking collectives: 38.1 us -> 40 us
  between operations: 3.2 us -> 1.34 us
    ppermute x11 -> x2, starting transfers between devices: 16.1 us -> 4.42 us  [per_device(): energy = energy + lax.ppermute(energy, ('contrast', 'pa'), pairs)]
    unnamed x26 -> x10, local copies, waits for them, and re-layouts: 9.15 us -> 0.03 us
    ppermute x11 -> x2, waiting for transfers between devices: 20 us -> 11.2 us  [per_device(): energy = energy + lax.ppermute(energy, ('contrast', 'pa'), pairs)]
    pallas_call x2, Pallas kernels: 12.5 us -> 15.9 us  [the longest x1 12.9 us: per_device(): pl.pallas_call(plane_kernel, grid=(coils,), out_shape=pltpu.HBM((parts, c...]
    pallas_call x1, Pallas kernels: 2.19 us -> 5.16 us  [per_device(): pl.pallas_call(z_forward_kernel, grid=(coils,), out_shape=buffer, in_spec...]
    all_to_all x1, blocking collectives: 38.1 us -> 40 us  [per_device(): lax.all_to_all(residual, ('pa', 'pb'), split_axis=0, concat_axis=0, tiled...]
  transfers between devices with their start and end apart: 12 -> 3, of which waited for: 9 -> 3; matrix products, arithmetic and copies ran while one was open for 0% -> 0% of each run, Pallas kernels for 0% -> 0%
where the time goes in v1:
time: 123 us
  waiting for transfers between devices  45.9 us (37%)
  blocking collectives  40 us (33%)
  Pallas kernels  21 us (17%)
  starting transfers between devices  13 us (11%)
  between operations  1.34 us (1%)
    all_to_all x1, blocking collectives, per_device(): lax.all_to_all(residual, ('pa', 'pb'), split_axis=0, concat_axis=0, tiled...  40 us
    all_to_all x1, waiting for transfers between devices, per_device(): lax.all_to_all(forward, ('pa', 'pb'), split_axis=0, concat_axis=0, tiled=...  34.7 us
    pallas_call x1, Pallas kernels, per_device(): pl.pallas_call(plane_kernel, grid=(coils,), out_shape=pltpu.HBM((parts, c...  12.9 us
    ppermute x2, waiting for transfers between devices, per_device(): energy = energy + lax.ppermute(energy, ('contrast', 'pa'), pairs)  11.2 us
    all_to_all x1, starting transfers between devices, per_device(): lax.all_to_all(forward, ('pa', 'pb'), split_axis=0, concat_axis=0, tiled=...  8.55 us
    pallas_call x1, Pallas kernels, per_device(): pl.pallas_call(z_forward_kernel, grid=(coils,), out_shape=buffer, in_spec...  5.16 us
    ppermute x2, starting transfers between devices, per_device(): energy = energy + lax.ppermute(energy, ('contrast', 'pa'), pairs)  4.42 us
    pallas_call x1, Pallas kernels, per_device(): pl.pallas_call(functools.partial(z_inverse_kernel, scale, coils), grid=(t...  2.96 us
  transfers between devices with their start and end apart: 3, of which 3 were waited for; matrix products, arithmetic and copies ran while one was open for 0% of the time, Pallas kernels for 0%

profile of v1, /device:TPU:0, one launch (start us, length us, event | category | flops | bytes accessed | tf_op | source)
XLA Modules:
  0.0 122.9 jit_solution(2283754640805866805)
XLA Ops:
  0.6 5.2 %shard_map.122 = f32[32,4,5,8,128]{4,3,2,1,0:T(8,128)} custom-call(f32[2,10,64,128]{3,2,1,0:T(8,128)} %bitcast.15, bf16[4,2,10,64,128]{4,3,2,1,0:T(8,128)(2,1)} %bitcast.13, bf16[256,768]{1,0:T(8,128)(2,1)} %constant.18.clone.table_ref), custom_call_target="tpu_custom_call" | custom-call | tf_op jit(solution)/shard_map/pallas_call | solution.py:291
  5.8 0.0 copy-start.2
  5.8 0.0 copy-start.3
  5.8 8.5 %all-to-all-start = ((f32[32,4,5,8,128]{4,3,2,1,0:T(8,128)}), f32[32,4,5,8,128]{4,3,2,1,0:T(8,128)S(1)}, u32[]{:S(2)}, u32[]{:S(2)}) async-start(f32[32,4,5,8,128]{4,3,2,1,0:T(8,128)} %shard_map.122), calls=%async_computation | async-start | bytes 5242880 | tf_op jit(solution)/shard_map/all_to_all | solution.py:303
  15.0 34.7 %all-to-all-done.in_ref = f32[32,4,5,8,128]{4,3,2,1,0:T(8,128)S(1)} async-done(((f32[32,4,5,8,128]{4,3,2,1,0:T(8,128)}), f32[32,4,5,8,128]{4,3,2,1,0:T(8,128)S(1)}, u32[]{:S(2)}, u32[]{:S(2)}) %all-to-all-start) | async-done | bytes 2621472 | tf_op jit(solution)/shard_map/all_to_all | solution.py:303
  49.7 0.0 copy-done.2
  49.7 0.0 copy-done.3
  49.7 12.9 %shard_map.123 = f32[32,21,8,128]{3,2,1,0:T(8,128)} custom-call(s32[1]{0:T(128)S(6)} %copy.13.present_ref, f32[32,4,5,8,128]{4,3,2,1,0:T(8,128)S(1)} %all-to-all-done.in_ref, bf16[768,256]{1,0:T(8,128)(2,1)S(1)} %copy-done.2, bf16[768,256]{1,0:T(8,128)(2,1)S(1)} %copy-done.3, bf16[4,2,4,160,128]{4,3,2,1,0:T(8,128)(2,1)} %bitcast.18, ...), custom_call_target="tpu_custom_call" | custom-call | tf_op jit(solution)/shard_map/pallas_call | solution.py:305
  62.6 0.0 copy-start
  62.6 0.0 copy-start.1
  62.6 0.0 copy-start.4
  62.6 40.0 %all_to_all.10.refs_0_.refs_1_.refs_2_.refs_3_.refs_4_ = f32[32,21,8,128]{3,2,1,0:T(8,128)S(1)} all-to-all(f32[32,21,8,128]{3,2,1,0:T(8,128)} %shard_map.123), channel_id=1, replica_groups=mesh['contrast'=4,'pa'=2,'pb'=16] {'pa','pb'}, dimensions={0} | all-to-all | bytes 5505024 | tf_op jit(solution)/shard_map/all_to_all | solution.py:324
  102.6 0.0 copy-done
  102.6 0.0 copy-done.1
  102.6 0.0 copy-done.4
  102.6 3.0 %shard_map.124 = (f32[2,10,64,128]{3,2,1,0:T(8,128)S(1)}, f32[81,8,128]{2,1,0:T(8,128)S(1)}) custom-call(s32[1]{0:T(128)S(6)} %copy.13.present_ref, f32[32,21,8,128]{3,2,1,0:T(8,128)S(1)} %all_to_all.10.refs_0_.refs_1_.refs_2_.refs_3_.refs_4_, f32[32,21,8,128]{3,2,1,0:T(8,128)S(1)} %all_to_all.10.refs_0_.refs_1_.refs_2_.refs_3_.refs_4_, ...), custom_call_target="tpu_custom_call" | custom-call | tf_op jit(solution)/shard_map/pallas_call | solution.py:335
  105.6 1.6 %collective-permute-start = (f32[81,8,128]{2,1,0:T(8,128)S(1)}, f32[81,8,128]{2,1,0:T(8,128)S(1)}, u32[]{:S(2)}, u32[]{:S(2)}) collective-permute-start(f32[81,8,128]{2,1,0:T(8,128)S(1)} %get-tuple-element.5), channel_id=1, source_target_pairs={{0,32},{32,0},{64,96},{96,64},{48,80},{80,48},{112,16},{16,112},{1... | collective-permute-start | bytes 995336 | tf_op jit(solution)/shard_map/ppermute | solution.py:365
  107.2 5.6 %collective-permute-done = f32[81,8,128]{2,1,0:T(8,128)S(1)} collective-permute-done((f32[81,8,128]{2,1,0:T(8,128)S(1)}, f32[81,8,128]{2,1,0:T(8,128)S(1)}, u32[]{:S(2)}, u32[]{:S(2)}) %collective-permute-start) | collective-permute-done | bytes 331808 | tf_op jit(solution)/shard_map/ppermute | solution.py:365
  112.9 2.8 %collective-permute-start.1 = (f32[81,8,128]{2,1,0:T(8,128)S(1)}, f32[81,8,128]{2,1,0:T(8,128)S(1)}, u32[]{:S(2)}, u32[]{:S(2)}) collective-permute-start(f32[81,8,128]{2,1,0:T(8,128)S(1)} %add.12), channel_id=1, source_target_pairs={{32,64},{64,32},{96,0},{0,96},{16,48},{48,16},{80,112},{112,80},{3... | collective-permute-start | bytes 995336 | tf_op jit(solution)/shard_map/ppermute | solution.py:365
  115.7 5.6 %collective-permute-done.1 = f32[81,8,128]{2,1,0:T(8,128)S(1)} collective-permute-done((f32[81,8,128]{2,1,0:T(8,128)S(1)}, f32[81,8,128]{2,1,0:T(8,128)S(1)}, u32[]{:S(2)}, u32[]{:S(2)}) %collective-permute-start.1) | collective-permute-done | bytes 331808 | tf_op jit(solution)/shard_map/ppermute | solution.py:365
  121.3 0.5 slice.9
  121.8 0.1 divide_multiply_fusion
  122.0 0.9 multiply_bitcast_fusion
  (2 shorter events, 0.1 us)
Async XLA Ops:
  5.8 43.9 %copy-start.2 = (bf16[768,256]{1,0:T(8,128)(2,1)S(1)}, bf16[768,256]{1,0:T(8,128)(2,1)}, u32[]{:S(2)}) copy-start(bf16[768,256]{1,0:T(8,128)(2,1)} %constant.20.clone.xf_ref) | copy-start | bytes 1179652
  5.8 43.9 %copy-start.3 = (bf16[768,256]{1,0:T(8,128)(2,1)S(1)}, bf16[768,256]{1,0:T(8,128)(2,1)}, u32[]{:S(2)}) copy-start(bf16[768,256]{1,0:T(8,128)(2,1)} %constant.21.clone.xi_ref) | copy-start | bytes 1179652
  5.8 43.9 %all-to-all-start = ((f32[32,4,5,8,128]{4,3,2,1,0:T(8,128)}), f32[32,4,5,8,128]{4,3,2,1,0:T(8,128)S(1)}, u32[]{:S(2)}, u32[]{:S(2)}) async-start(f32[32,4,5,8,128]{4,3,2,1,0:T(8,128)} %shard_map.122), calls=%async_computation | async-start | bytes 5242880 | tf_op jit(solution)/shard_map/all_to_all | solution.py:303
  62.6 40.0 %copy-start = (bf16[4,2,64,10,128]{4,2,3,1,0:T(8,128)(2,1)S(1)}, bf16[4,2,64,10,128]{4,2,3,1,0:T(8,128)(2,1)}, u32[]{:S(2)}) copy-start(bf16[4,2,64,10,128]{4,2,3,1,0:T(8,128)(2,1)} %param.12) | copy-start | bytes 3932164
  62.6 40.0 %copy-start.1 = (f32[1,2,64,10,128]{4,2,3,1,0:T(8,128)S(1)}, f32[1,2,64,10,128]{4,2,3,1,0:T(8,128)}, u32[]{:S(2)}) copy-start(f32[1,2,64,10,128]{4,2,3,1,0:T(8,128)} %param.11) | copy-start | bytes 1966084
  62.6 40.0 %copy-start.4 = (bf16[768,256]{1,0:T(8,128)(2,1)S(1)}, bf16[768,256]{1,0:T(8,128)(2,1)}, u32[]{:S(2)}) copy-start(bf16[768,256]{1,0:T(8,128)(2,1)} %constant.19.clone.refs_7_) | copy-start | bytes 1179652
  105.6 7.2 %collective-permute-start = (f32[81,8,128]{2,1,0:T(8,128)S(1)}, f32[81,8,128]{2,1,0:T(8,128)S(1)}, u32[]{:S(2)}, u32[]{:S(2)}) collective-permute-start(f32[81,8,128]{2,1,0:T(8,128)S(1)} %get-tuple-element.5), channel_id=1, source_target_pairs={{0,32},{32,0},{64,96},{96,64},{48,80},{80,48},{112,16},{16,112},{1... | collective-permute-start | bytes 995336 | tf_op jit(solution)/shard_map/ppermute | solution.py:365
  112.9 8.4 %collective-permute-start.1 = (f32[81,8,128]{2,1,0:T(8,128)S(1)}, f32[81,8,128]{2,1,0:T(8,128)S(1)}, u32[]{:S(2)}, u32[]{:S(2)}) collective-permute-start(f32[81,8,128]{2,1,0:T(8,128)S(1)} %add.12), channel_id=1, source_target_pairs={{32,64},{64,32},{96,0},{0,96},{16,48},{48,16},{80,112},{112,80},{3... | collective-permute-start | bytes 995336 | tf_op jit(solution)/shard_map/ppermute | solution.py:365

commit v2 on v0

v2 whole, which is shorter than its diff:
```python
import functools
import math

import jax
import jax.numpy as jnp
import ml_dtypes
import numpy as np
from jax import lax
from jax.experimental import pallas as pl
from jax.experimental.pallas import tpu as pltpu
from jax.sharding import PartitionSpec as P

step_size = 1.0
threshold = 2.5
LANES = 128
VMEM_LIMIT = 40 * 1024 * 1024


def trig(length):
    index = np.arange(length)
    angles = (index[:, None] * index[None, :] % length) * (2.0 * math.pi / length)
    scale = 1.0 / math.sqrt(length)
    return np.cos(angles) * scale, np.sin(angles) * scale


def halves(table):
    high = table.astype(np.float32).astype(ml_dtypes.bfloat16)
    low = (table - high.astype(np.float64)).astype(np.float32).astype(ml_dtypes.bfloat16)
    return high, low


def left_table(table):
    high, low = halves(table)
    return np.concatenate([high, high, low], axis=1)


def right_table(table):
    high, low = halves(table)
    return np.concatenate([high, high, low], axis=0)


def split_data(value, axis):
    high = value.astype(jnp.bfloat16)
    low = (value - high.astype(jnp.float32)).astype(jnp.bfloat16)
    return jnp.concatenate([high, low, high], axis=axis)


def dot(left, right, dims):
    return lax.dot_general(left, right, (dims, ((), ())), preferred_element_type=jnp.float32)


def z_forward_table(depth):
    c, s = trig(depth)
    re_row = np.concatenate([c, s], axis=1)
    im_row = np.concatenate([-s, c], axis=1)
    return left_table(np.stack([re_row, im_row], axis=1).reshape(2 * depth, 2 * depth))


def z_inverse_table(depth):
    c, s = trig(depth)
    re_row = np.concatenate([c, s], axis=1)
    im_row = np.concatenate([-s, c], axis=1)
    return right_table(np.stack([re_row, im_row], axis=1).reshape(2 * depth, 2 * depth))


def x_table(width, sign):
    c, s = trig(width)
    s = sign * s
    return right_table(np.concatenate([np.concatenate([c, s], 1), np.concatenate([-s, c], 1)], 0))


def y_order(groups, rows):
    y = np.arange(groups * rows).reshape(groups, rows // 2, 2)
    return y.transpose(2, 1, 0).reshape(-1)


def y_tables(width, order, parity):
    c, s = trig(width)
    half = width // 2
    y = order[parity * half : (parity + 1) * half]
    forward = np.concatenate([c[:half, y], s[:half, y]], axis=0)
    back = np.concatenate([c[y, :half], s[y, :half]], axis=0)
    return left_table(forward), left_table(back)


def z_forward_kernel(
    group, present_ref, image_hbm, maps_hbm, table_hbm, out_ref, image_ref, maps_ref, table_ref, sems
):
    coils = maps_ref.shape[0]
    rows = image_ref.shape[1] * image_ref.shape[2]
    depth = image_ref.shape[3]
    tiles = rows // LANES
    parts, _, sub, _ = out_ref.shape
    copies = [
        pltpu.make_async_copy(image_hbm, image_ref, sems.at[0]),
        pltpu.make_async_copy(table_hbm, table_ref, sems.at[1]),
    ]
    for coil in range(coils):
        copies.append(
            pltpu.make_async_copy(maps_hbm.at[coil], maps_ref.at[coil], sems.at[2 + coil])
        )
    first = [copies[0], copies[2], copies[1]] + copies[3:]
    for copy in first:
        copy.start()
    copies[0].wait()
    image_re = image_ref[0].reshape(rows, depth)
    image_im = image_ref[1].reshape(rows, depth)
    for start in range(0, coils, group):
        pieces = []
        for coil in range(start, start + group):
            copies[2 + coil].wait()
            maps_re = maps_ref[coil, 0].reshape(rows, depth).astype(jnp.float32)
            maps_im = maps_ref[coil, 1].reshape(rows, depth).astype(jnp.float32)
            product = jnp.concatenate(
                [
                    maps_re * image_re - maps_im * image_im,
                    maps_re * image_im + maps_im * image_re,
                ],
                axis=1,
            )
            pieces.append(split_data(product, 1))
        if start == 0:
            copies[1].wait()
        result = dot(table_ref[...], jnp.concatenate(pieces, axis=0), ((1,), (1,)))
        for tile in range(group * tiles):
            out_ref[:, start * tiles + tile] = result[
                :, tile * LANES : (tile + 1) * LANES
            ].reshape(parts, sub, LANES)


def plane_kernel(
    group, present_ref, in_ref, xf_ref, xi_ref, kspace_ref, sampling_ref, yfe_ref, yfo_ref, yie_ref,
    yio_ref, out_ref,
):
    parts, _, sub, _ = in_ref.shape
    coils = kspace_ref.shape[0]
    tiles = in_ref.shape[1] // coils
    planes = sub // 2
    along = parts // 2
    rows = along * tiles
    width_y = kspace_ref.shape[3]
    present = present_ref[0].astype(jnp.float32)
    half = LANES // 2
    low_lanes = lax.broadcasted_iota(jnp.int32, (rows, LANES), 1) < half
    in_stride = in_ref.shape[1] * sub
    out_stride = out_ref.shape[1] * sub
    flat_in = in_ref.reshape(parts * in_stride, LANES)
    flat_out = out_ref.reshape(parts * out_stride, LANES)

    def interleave(first, second):
        even = jnp.where(low_lanes, first, pltpu.roll(second, half, 1))
        odd = jnp.where(low_lanes, pltpu.roll(first, half, 1), second)
        return even, odd

    def gather(side, coil, at):
        base = side * along * in_stride + coil * tiles * sub + at
        return jnp.concatenate(
            [flat_in[pl.ds(base + t * sub, along, stride=in_stride), :] for t in range(tiles)], axis=0
        )

    def scatter(side, coil, at, value):
        base = side * along * out_stride + coil * tiles * sub + at
        for t in range(tiles):
            flat_out[pl.ds(base + t * sub, along, stride=out_stride), :] = value[
                t * along : (t + 1) * along
            ]

    def pick(value, plane, part):
        at = (2 * plane + part) * LANES
        return value[:, at : at + LANES]

    def forward(table_ref, data):
        both = dot(table_ref[...], split_data(data, 0), ((1,), (0,)))
        c, s = both[:rows], both[rows:]
        return [
            (pick(c, p, 0) + pick(s, p, 1), pick(c, p, 1) - pick(s, p, 0)) for p in range(planes)
        ]

    def backward(table_ref, data):
        both = dot(table_ref[...], split_data(data, 0), ((1,), (0,)))
        c, s = both[:rows], both[rows:]
        return [
            (pick(c, p, 0) - pick(s, p, 1), pick(c, p, 1) + pick(s, p, 0)) for p in range(planes)
        ]

    total = jnp.zeros((8, LANES), jnp.float32)
    for start in range(0, coils, group):
        members = range(start, start + group)
        gathered = []
        for coil in members:
            for plane in range(planes):
                sides = []
                for part in range(2):
                    at = 2 * plane + part
                    sides.append(
                        jnp.concatenate(
                            interleave(gather(0, coil, at), gather(1, coil, at)), axis=0
                        )
                    )
                gathered.append(jnp.concatenate(sides, axis=1))
        after_x = dot(split_data(jnp.concatenate(gathered, axis=0), 1), xf_ref[...], ((1,), (0,)))
        back = []
        for n, coil in enumerate(members):
            at = [(n * planes + plane) * width_y for plane in range(planes)]
            even = forward(yfe_ref, jnp.concatenate([after_x[a : a + rows] for a in at], axis=1))
            odd = forward(
                yfo_ref, jnp.concatenate([after_x[a + rows : a + width_y] for a in at], axis=1)
            )
            sums, gaps = [], []
            for plane in range(planes):
                weight = sampling_ref[plane].astype(jnp.float32) * present
                for part in range(2):
                    measured = kspace_ref[coil, part, plane].astype(jnp.float32)
                    e, o = even[plane][part], odd[plane][part]
                    low = weight[:rows] * ((e + o) - measured[:rows])
                    high = weight[rows:] * ((e - o) - measured[rows:])
                    square = low * low + high * high
                    total = total + jnp.sum(square.reshape(rows // 8, 8, LANES), axis=0)
                    sums.append(low + high)
                    gaps.append(low - high)
            even = backward(yie_ref, jnp.concatenate(sums, axis=1))
            odd = backward(yio_ref, jnp.concatenate(gaps, axis=1))
            for plane in range(planes):
                back.append(jnp.concatenate(even[plane], axis=1))
                back.append(jnp.concatenate(odd[plane], axis=1))
        returned = dot(split_data(jnp.concatenate(back, axis=0), 1), xi_ref[...], ((1,), (0,)))
        for n, coil in enumerate(members):
            for plane in range(planes):
                a = (n * planes + plane) * width_y
                for part in range(2):
                    block = returned[a : a + width_y, part * LANES : (part + 1) * LANES]
                    first, second = interleave(block[:rows], block[rows:])
                    scatter(0, coil, 2 * plane + part, first)
                    scatter(1, coil, 2 * plane + part, second)
    out_ref[:, coils * tiles] = jnp.broadcast_to(total[None], (parts, sub, LANES))


def z_inverse_kernel(
    scale, present_ref, in_ref, maps_ref, image_ref, table_ref, moved_ref, energy_ref
):
    parts, _, sub, _ = in_ref.shape
    coils = maps_ref.shape[0]
    _, y_rows, x_rows, depth = image_ref.shape
    rows = y_rows * x_rows
    tiles = rows // LANES
    present = present_ref[0].astype(jnp.float32)
    grad_re = jnp.zeros((rows, depth), jnp.float32)
    grad_im = jnp.zeros((rows, depth), jnp.float32)
    for coil in range(coils):
        data = jnp.concatenate(
            [in_ref[:, coil * tiles + t].reshape(parts * sub, LANES) for t in range(tiles)], axis=1
        )
        result = dot(split_data(data, 0), table_ref[...], ((0,), (0,)))
        back_re = result[:, :depth]
        back_im = result[:, depth:]
        maps_re = maps_ref[coil, 0].reshape(rows, depth).astype(jnp.float32)
        maps_im = maps_ref[coil, 1].reshape(rows, depth).astype(jnp.float32)
        grad_re = grad_re + (maps_re * back_re + maps_im * back_im)
        grad_im = grad_im + (maps_re * back_im - maps_im * back_re)
    shape = image_ref.shape[1:]
    moved_re = image_ref[0] - step_size * grad_re.reshape(shape)
    moved_im = image_ref[1] - step_size * grad_im.reshape(shape)
    moved_ref[0] = moved_re
    moved_ref[1] = moved_im
    energy = present * (moved_re * moved_re + moved_im * moved_im)
    energy_ref[: rows // 8] = energy.reshape(rows // 8, 8, depth)
    misfit = jnp.sum(in_ref[:, coils * tiles], axis=0)
    energy_ref[rows // 8] = jnp.full((8, depth), jnp.sum(misfit) * scale)


def params():
    return pltpu.CompilerParams(vmem_limit_bytes=VMEM_LIMIT)


def in_vmem(array):
    return pltpu.with_memory_space_constraint(array, pltpu.VMEM)


def in_hbm(array):
    return pltpu.with_memory_space_constraint(array, pltpu.HBM)


def per_device(image, coil_maps, kspace, sampling, available):
    pa = lax.axis_size("pa")
    pb = lax.axis_size("pb")
    pixels = jnp.transpose(image[0], (0, 2, 1, 3))
    maps = jnp.transpose(coil_maps, (0, 1, 3, 2, 4))
    samples = kspace[0]
    mask = sampling[0]
    _, y_rows, x_rows, depth = pixels.shape
    coils = maps.shape[0]
    parts = pa * pb
    sub = 2 * depth // parts
    tiles = y_rows * x_rows // LANES
    width_x = x_rows * pa
    width_y = y_rows * pb
    order = y_order(pb, y_rows)
    zf = jnp.asarray(z_forward_table(depth))
    zi = jnp.asarray(z_inverse_table(depth))
    xf = jnp.asarray(x_table(width_x, -1.0))
    xi = jnp.asarray(x_table(width_x, 1.0))
    (yfe, yie), (yfo, yio) = (y_tables(width_y, order, parity) for parity in range(2))
    yfe, yie, yfo, yio = (jnp.asarray(table) for table in (yfe, yie, yfo, yio))
    scalar = pl.BlockSpec(memory_space=pltpu.SMEM)
    anywhere = pl.BlockSpec(memory_space=pl.ANY)
    local = pl.BlockSpec(memory_space=pltpu.VMEM)
    forward = pl.pallas_call(
        functools.partial(z_forward_kernel, 2 if coils % 2 == 0 else 1),
        out_shape=jax.ShapeDtypeStruct((parts, coils * tiles, sub, LANES), jnp.float32),
        in_specs=[scalar, anywhere, anywhere, anywhere],
        out_specs=local,
        scratch_shapes=[
            pltpu.VMEM(pixels.shape, pixels.dtype),
            pltpu.VMEM(maps.shape, maps.dtype),
            pltpu.VMEM(zf.shape, zf.dtype),
            pltpu.SemaphoreType.DMA((2 + coils,)),
        ],
        compiler_params=params(),
    )(available, in_hbm(pixels), in_hbm(maps), in_hbm(zf))
    received = lax.all_to_all(forward, ("pa", "pb"), split_axis=0, concat_axis=0, tiled=True)
    residual = pl.pallas_call(
        functools.partial(plane_kernel, coils),
        out_shape=jax.ShapeDtypeStruct((parts, coils * tiles + 1, sub, LANES), jnp.float32),
        in_specs=[scalar] + [local] * 9,
        out_specs=local,
        compiler_params=params(),
    )(
        available, received, xf, xi, in_vmem(samples), in_vmem(mask),
        in_vmem(yfe), in_vmem(yfo), in_vmem(yie), in_vmem(yio),
    )
    returned = lax.all_to_all(residual, ("pa", "pb"), split_axis=0, concat_axis=0, tiled=True)

    contrasts = lax.axis_size("contrast") * image.shape[0]
    scale = 1.0 / (2.0 * contrasts * coils * width_x * width_y * depth)
    energy_tiles = y_rows * x_rows // 8
    moved, energy = pl.pallas_call(
        functools.partial(z_inverse_kernel, scale),
        out_shape=(
            jax.ShapeDtypeStruct(pixels.shape, jnp.float32),
            jax.ShapeDtypeStruct((energy_tiles + 1, 8, depth), jnp.float32),
        ),
        in_specs=[scalar] + [local] * 4,
        out_specs=(local, local),
        compiler_params=params(),
    )(available, returned, maps, pixels, zi)

    size = lax.axis_size("contrast")
    for step in range(2):
        pairs = []
        for core in range(pa):
            shift = (core + step) % 2
            for low in range(shift, size + shift, 2):
                first, second = low % size * pa + core, (low + 1) % size * pa + core
                pairs += [(first, second), (second, first)]
        energy = energy + lax.ppermute(energy, ("contrast", "pa"), pairs)
    norm_value = jnp.sqrt(energy[:energy_tiles].reshape(y_rows, x_rows, depth))
    present = available[0].astype(jnp.float32)
    factor = jnp.maximum(norm_value - threshold, 0.0) / jnp.maximum(norm_value, threshold)
    shrink = present * factor
    result = jnp.transpose(moved * shrink[None], (0, 2, 1, 3))[None]
    return (result, energy[energy_tiles, 0, 0])


def solution(mesh):
    return jax.shard_map(
        per_device,
        mesh=mesh,
        in_specs=(
            P("contrast", None, "pa", "pb", None),
            P(None, None, "pa", "pb", None),
            P("contrast", None, None, ("pa", "pb"), None, None),
            P("contrast", ("pa", "pb"), None, None),
            P("contrast"),
        ),
        out_specs=(P("contrast", None, "pa", "pb", None), P()),
        check_vma=False,
    )
```

time: 147 us -> 113 us (0.77)
  blocking collectives: 38.1 us -> 81.8 us
  waiting for transfers between devices: 54.7 us -> 11.2 us
  starting transfers between devices: 24.6 us -> 4.41 us
  local copies, waits for them, and re-layouts: 9.15 us -> 0.59 us
  Pallas kernels: 14.7 us -> 11.7 us
  between operations: 3.2 us -> 1.44 us
    all_to_all x0 -> x1, blocking collectives: none -> 42.8 us  [per_device(): lax.all_to_all(forward, ('pa', 'pb'), split_axis=0, concat_axis=0, tiled=...]
    all_to_all x1 -> x0, waiting for transfers between devices: 34.7 us -> none  [per_device(): lax.all_to_all(forward, ('pa', 'pb'), split_axis=0, concat_axis=0, tiled=...]
    ppermute x11 -> x2, starting transfers between devices: 16.1 us -> 4.41 us  [per_device(): energy = energy + lax.ppermute(energy, ('contrast', 'pa'), pairs)]
    unnamed x26 -> x22, local copies, waits for them, and re-layouts: 9.15 us -> 0.07 us
    ppermute x11 -> x2, waiting for transfers between devices: 20 us -> 11.2 us  [per_device(): energy = energy + lax.ppermute(energy, ('contrast', 'pa'), pairs)]
    all_to_all x1 -> x0, starting transfers between devices: 8.55 us -> none  [per_device(): lax.all_to_all(forward, ('pa', 'pb'), split_axis=0, concat_axis=0, tiled=...]
    pallas_call x3, Pallas kernels: 14.7 us -> 11.7 us  [the longest x1 6.58 us: per_device(): pl.pallas_call(functools.partial(plane_kernel, coils), out_shape=jax.Shap...]
  transfers between devices with their start and end apart: 12 -> 2, of which waited for: 9 -> 2; matrix products, arithmetic and copies ran while one was open for 0% -> 0% of each run, Pallas kernels for 0% -> 0%
where the time goes in v2:
time: 113 us; the launch traced here: 112 us
  blocking collectives  81.8 us (72%)
  Pallas kernels  11.7 us (10%)
  waiting for transfers between devices  11.2 us (10%)
  starting transfers between devices  4.41 us (4%)
  between operations  1.44 us (1%)
  other arithmetic  1.15 us (1%)
    all_to_all x1, blocking collectives, per_device(): lax.all_to_all(forward, ('pa', 'pb'), split_axis=0, concat_axis=0, tiled=...  42.8 us
    all_to_all x1, blocking collectives, per_device(): lax.all_to_all(residual, ('pa', 'pb'), split_axis=0, concat_axis=0, tiled...  39 us
    ppermute x2, waiting for transfers between devices, per_device(): energy = energy + lax.ppermute(energy, ('contrast', 'pa'), pairs)  11.2 us
    pallas_call x1, Pallas kernels, per_device(): pl.pallas_call(functools.partial(plane_kernel, coils), out_shape=jax.Shap...  6.58 us
    ppermute x2, starting transfers between devices, per_device(): energy = energy + lax.ppermute(energy, ('contrast', 'pa'), pairs)  4.41 us
    pallas_call x1, Pallas kernels, per_device(): pl.pallas_call(functools.partial(z_forward_kernel, 2 if coils % 2 == 0 el...  3.72 us
  transfers between devices with their start and end apart: 2, of which 2 were waited for; matrix products, arithmetic and copies ran while one was open for 0% of the time, Pallas kernels for 0%

profile of v2, /device:TPU:0, one launch (start us, length us, event | category | flops | bytes accessed | tf_op | source)
XLA Modules:
  0.0 112.3 jit_solution(15572730111756087961)
XLA Ops:
  1.3 3.7 %shard_map.140 = f32[32,20,8,128]{3,2,1,0:T(8,128)S(1)} custom-call(s32[1]{0:T(128)S(6)} %copy.15.present_ref, f32[2,10,64,128]{3,2,1,0:T(8,128)} %bitcast.15, bf16[4,2,10,64,128]{4,3,2,1,0:T(8,128)(2,1)} %bitcast.13, bf16[256,768]{1,0:T(8,128)(2,1)} %constant.22.clone.table_hbm), custom_call_target="tpu_custom_call" | custom-call | tf_op jit(solution)/shard_map/pallas_call | solution.py:307
  5.0 0.0 copy-start.2
  5.0 0.0 copy-start.3
  5.0 0.0 copy-start.4
  5.0 0.0 copy-start.6
  5.1 0.0 copy-start.7
  5.1 0.0 copy-start.8
  5.1 0.0 copy-start.9
  5.1 0.0 copy-start.10
  5.1 42.8 %all_to_all.10.in_ref = f32[32,20,8,128]{3,2,1,0:T(8,128)S(1)} all-to-all(f32[32,20,8,128]{3,2,1,0:T(8,128)S(1)} %shard_map.140), channel_id=1, replica_groups=mesh['contrast'=4,'pa'=2,'pb'=16] {'pa','pb'}, dimensions={0} | all-to-all | bytes 5242880 | tf_op jit(solution)/shard_map/all_to_all | solution.py:320
  47.9 0.0 copy-done.2
  47.9 0.0 copy-done.3
  47.9 0.0 copy-done.4
  47.9 0.0 copy-done.6
  47.9 0.0 copy-done.7
  47.9 0.0 copy-done.8
  47.9 0.0 copy-done.9
  47.9 0.0 copy-done.10
  48.0 6.6 %shard_map.141 = f32[32,21,8,128]{3,2,1,0:T(8,128)S(1)} custom-call(s32[1]{0:T(128)S(6)} %copy.15.present_ref, f32[32,20,8,128]{3,2,1,0:T(8,128)S(1)} %all_to_all.10.in_ref, bf16[768,256]{1,0:T(8,128)(2,1)S(1)} %copy-done.3, bf16[768,256]{1,0:T(8,128)(2,1)S(1)} %copy-done.4, bf16[4,2,4,160,128]{4,3,2,1,0:T(8,128)(2,1)S(1)} %bitcast.17, ...), custom_call_target="tpu_custom_call" | custom-call | tf_op jit(solution)/shard_map/pallas_call | solution.py:321
  54.5 0.0 copy-start
  54.6 0.0 copy-start.1
  54.6 0.0 copy-start.5
  54.6 39.0 %all_to_all.11.in_ref = f32[32,21,8,128]{3,2,1,0:T(8,128)S(1)} all-to-all(f32[32,21,8,128]{3,2,1,0:T(8,128)S(1)} %shard_map.141), channel_id=1, replica_groups=mesh['contrast'=4,'pa'=2,'pb'=16] {'pa','pb'}, dimensions={0} | all-to-all | bytes 5505024 | tf_op jit(solution)/shard_map/all_to_all | solution.py:331
  93.6 0.0 copy-done
  93.6 0.0 copy-done.1
  93.6 0.0 copy-done.5
  93.6 1.4 %shard_map.142 = (f32[2,10,64,128]{3,2,1,0:T(8,128)S(1)}, f32[81,8,128]{2,1,0:T(8,128)S(1)}) custom-call(s32[1]{0:T(128)S(6)} %copy.15.present_ref, f32[32,21,8,128]{3,2,1,0:T(8,128)S(1)} %all_to_all.11.in_ref, bf16[4,2,10,64,128]{4,3,2,1,0:T(8,128)(2,1)S(1)} %bitcast.14, f32[2,10,64,128]{3,2,1,0:T(8,128)S(1)} %bitcast.16, bf16[768,256]{1,0:T(8,128)(2,1)S(1)} %copy-done.5), custom_call_target="tpu_custom_call" | custom-call | tf_op jit(solution)/shard_map/pallas_call | solution.py:336
  95.1 1.6 %collective-permute-start = (f32[81,8,128]{2,1,0:T(8,128)S(1)}, f32[81,8,128]{2,1,0:T(8,128)S(1)}, u32[]{:S(2)}, u32[]{:S(2)}) collective-permute-start(f32[81,8,128]{2,1,0:T(8,128)S(1)} %get-tuple-element.5), channel_id=1, source_target_pairs={{0,32},{32,0},{64,96},{96,64},{48,80},{80,48},{112,16},{16,112},{1... | collective-permute-start | bytes 995336 | tf_op jit(solution)/shard_map/ppermute | solution.py:355
  96.6 5.6 %collective-permute-done = f32[81,8,128]{2,1,0:T(8,128)S(1)} collective-permute-done((f32[81,8,128]{2,1,0:T(8,128)S(1)}, f32[81,8,128]{2,1,0:T(8,128)S(1)}, u32[]{:S(2)}, u32[]{:S(2)}) %collective-permute-start) | collective-permute-done | bytes 331808 | tf_op jit(solution)/shard_map/ppermute | solution.py:355
  102.3 2.8 %collective-permute-start.1 = (f32[81,8,128]{2,1,0:T(8,128)S(1)}, f32[81,8,128]{2,1,0:T(8,128)S(1)}, u32[]{:S(2)}, u32[]{:S(2)}) collective-permute-start(f32[81,8,128]{2,1,0:T(8,128)S(1)} %add.12), channel_id=1, source_target_pairs={{32,64},{64,32},{96,0},{0,96},{16,48},{48,16},{80,112},{112,80},{3... | collective-permute-start | bytes 995336 | tf_op jit(solution)/shard_map/ppermute | solution.py:355
  105.1 5.6 %collective-permute-done.1 = f32[81,8,128]{2,1,0:T(8,128)S(1)} collective-permute-done((f32[81,8,128]{2,1,0:T(8,128)S(1)}, f32[81,8,128]{2,1,0:T(8,128)S(1)}, u32[]{:S(2)}, u32[]{:S(2)}) %collective-permute-start.1) | collective-permute-done | bytes 331808 | tf_op jit(solution)/shard_map/ppermute | solution.py:355
  110.8 0.5 slice.9
  111.3 0.1 divide_multiply_fusion
  111.4 0.9 multiply_bitcast_fusion
  (2 shorter events, 0.1 us)
Async XLA Ops:
  5.0 42.9 %copy-start.2 = (bf16[1,4,2,4,160,128]{5,4,3,2,1,0:T(8,128)(2,1)S(1)}, bf16[1,4,2,4,160,128]{5,4,3,2,1,0:T(8,128)(2,1)}, u32[]{:S(2)}) copy-start(bf16[1,4,2,4,160,128]{5,4,3,2,1,0:T(8,128)(2,1)} %param.15) | copy-start | bytes 3932164
  5.0 42.9 %copy-start.3 = (bf16[768,256]{1,0:T(8,128)(2,1)S(1)}, bf16[768,256]{1,0:T(8,128)(2,1)}, u32[]{:S(2)}) copy-start(bf16[768,256]{1,0:T(8,128)(2,1)} %constant.24.clone.xf_ref) | copy-start | bytes 1179652
  5.0 42.9 %copy-start.4 = (bf16[768,256]{1,0:T(8,128)(2,1)S(1)}, bf16[768,256]{1,0:T(8,128)(2,1)}, u32[]{:S(2)}) copy-start(bf16[768,256]{1,0:T(8,128)(2,1)} %constant.25.clone.xi_ref) | copy-start | bytes 1179652
  5.0 42.9 %copy-start.6 = (s32[1,4,160,128]{3,2,1,0:T(8,128)S(1)}, s32[1,4,160,128]{3,2,1,0:T(8,128)}, u32[]{:S(2)}) copy-start(s32[1,4,160,128]{3,2,1,0:T(8,128)} %param.16) | copy-start | bytes 983044
  5.1 42.9 %copy-start.7 = (bf16[160,240]{1,0:T(8,128)(2,1)S(1)}, bf16[160,240]{1,0:T(8,128)(2,1)}, u32[]{:S(2)}) copy-start(bf16[160,240]{1,0:T(8,128)(2,1)} %constant.26.clone.yfe_ref) | copy-start | bytes 230404
  5.1 42.9 %copy-start.8 = (bf16[160,240]{1,0:T(8,128)(2,1)S(1)}, bf16[160,240]{1,0:T(8,128)(2,1)}, u32[]{:S(2)}) copy-start(bf16[160,240]{1,0:T(8,128)(2,1)} %constant.27.clone.yie_ref) | copy-start | bytes 230404
  5.1 42.9 %copy-start.9 = (bf16[160,240]{1,0:T(8,128)(2,1)S(1)}, bf16[160,240]{1,0:T(8,128)(2,1)}, u32[]{:S(2)}) copy-start(bf16[160,240]{1,0:T(8,128)(2,1)} %constant.28.clone.yfo_ref) | copy-start | bytes 230404
  5.1 42.9 %copy-start.10 = (bf16[160,240]{1,0:T(8,128)(2,1)S(1)}, bf16[160,240]{1,0:T(8,128)(2,1)}, u32[]{:S(2)}) copy-start(bf16[160,240]{1,0:T(8,128)(2,1)} %constant.29.clone.yio_ref) | copy-start | bytes 230404
  54.5 39.1 %copy-start = (bf16[4,2,64,10,128]{4,2,3,1,0:T(8,128)(2,1)S(1)}, bf16[4,2,64,10,128]{4,2,3,1,0:T(8,128)(2,1)}, u32[]{:S(2)}) copy-start(bf16[4,2,64,10,128]{4,2,3,1,0:T(8,128)(2,1)} %param.14) | copy-start | bytes 3932164
  54.6 39.1 %copy-start.1 = (f32[1,2,64,10,128]{4,2,3,1,0:T(8,128)S(1)}, f32[1,2,64,10,128]{4,2,3,1,0:T(8,128)}, u32[]{:S(2)}) copy-start(f32[1,2,64,10,128]{4,2,3,1,0:T(8,128)} %param.13) | copy-start | bytes 1966084
  54.6 39.1 %copy-start.5 = (bf16[768,256]{1,0:T(8,128)(2,1)S(1)}, bf16[768,256]{1,0:T(8,128)(2,1)}, u32[]{:S(2)}) copy-start(bf16[768,256]{1,0:T(8,128)(2,1)} %constant.23.clone.table_ref) | copy-start | bytes 1179652
  95.1 7.2 %collective-permute-start = (f32[81,8,128]{2,1,0:T(8,128)S(1)}, f32[81,8,128]{2,1,0:T(8,128)S(1)}, u32[]{:S(2)}, u32[]{:S(2)}) collective-permute-start(f32[81,8,128]{2,1,0:T(8,128)S(1)} %get-tuple-element.5), channel_id=1, source_target_pairs={{0,32},{32,0},{64,96},{96,64},{48,80},{80,48},{112,16},{16,112},{1... | collective-permute-start | bytes 995336 | tf_op jit(solution)/shard_map/ppermute | solution.py:355
  102.3 8.4 %collective-permute-start.1 = (f32[81,8,128]{2,1,0:T(8,128)S(1)}, f32[81,8,128]{2,1,0:T(8,128)S(1)}, u32[]{:S(2)}, u32[]{:S(2)}) collective-permute-start(f32[81,8,128]{2,1,0:T(8,128)S(1)} %add.12), channel_id=1, source_target_pairs={{32,64},{64,32},{96,0},{0,96},{16,48},{48,16},{80,112},{112,80},{3... | collective-permute-start | bytes 995336 | tf_op jit(solution)/shard_map/ppermute | solution.py:355

commit v3 on v2

--- a/solution.py
+++ b/solution.py
@@ -13,6 +13,8 @@
 step_size = 1.0
 threshold = 2.5
 LANES = 128
+CHUNKS = 2
+Z_CHUNK = 2
 VMEM_LIMIT = 40 * 1024 * 1024
 
 
@@ -84,33 +86,45 @@
 
 
 def z_forward_kernel(
-    group, present_ref, image_hbm, maps_hbm, table_hbm, out_ref, image_ref, maps_ref, table_ref, sems
+    chunk, present_ref, image_hbm, maps_hbm, table_hbm, out_ref, image_ref, maps_ref, table_ref, sems
 ):
     coils = maps_ref.shape[0]
-    rows = image_ref.shape[1] * image_ref.shape[2]
-    depth = image_ref.shape[3]
-    tiles = rows // LANES
+    _, y_rows, x_rows, depth = image_ref.shape
+    pair = LANES // x_rows
     parts, _, sub, _ = out_ref.shape
-    copies = [
-        pltpu.make_async_copy(image_hbm, image_ref, sems.at[0]),
-        pltpu.make_async_copy(table_hbm, table_ref, sems.at[1]),
-    ]
-    for coil in range(coils):
+    tiles = y_rows // pair
+    table_copy = pltpu.make_async_copy(table_hbm, table_ref, sems.at[0])
+    copies = []
+    for t in range(0, tiles, chunk):
+        along = pl.ds(t * pair, min(chunk, tiles - t) * pair)
+        n = len(copies)
         copies.append(
-            pltpu.make_async_copy(maps_hbm.at[coil], maps_ref.at[coil], sems.at[2 + coil])
+            [
+                pltpu.make_async_copy(
+                    image_hbm.at[:, along], image_ref.at[:, along], sems.at[2 * n + 1]
+                ),
+                pltpu.make_async_copy(
+                    maps_hbm.at[:, :, along], maps_ref.at[:, :, along], sems.at[2 * n + 2]
+                ),
+            ]
         )
-    first = [copies[0], copies[2], copies[1]] + copies[3:]
-    for copy in first:
-        copy.start()
-    copies[0].wait()
-    image_re = image_ref[0].reshape(rows, depth)
-    image_im = image_ref[1].reshape(rows, depth)
-    for start in range(0, coils, group):
+    for n, both in enumerate(copies):
+        for copy in both:
+            copy.start()
+        if n == 0:
+            table_copy.start()
+    for n, both in enumerate(copies):
+        for copy in both:
+            copy.wait()
+        members = range(n * chunk, min((n + 1) * chunk, tiles))
+        along = pl.ds(members.start * pair, len(members) * pair)
+        rows = len(members) * LANES
+        image_re = image_ref[0, along].reshape(rows, depth)
+        image_im = image_ref[1, along].reshape(rows, depth)
         pieces = []
-        for coil in range(start, start + group):
-            copies[2 + coil].wait()
-            maps_re = maps_ref[coil, 0].reshape(rows, depth).astype(jnp.float32)
-            maps_im = maps_ref[coil, 1].reshape(rows, depth).astype(jnp.float32)
+        for coil in range(coils):
+            maps_re = maps_ref[coil, 0, along].reshape(rows, depth).astype(jnp.float32)
+            maps_im = maps_ref[coil, 1, along].reshape(rows, depth).astype(jnp.float32)
             product = jnp.concatenate(
                 [
                     maps_re * image_re - maps_im * image_im,
@@ -119,13 +133,13 @@
                 axis=1,
             )
             pieces.append(split_data(product, 1))
-        if start == 0:
-            copies[1].wait()
+        if n == 0:
+            table_copy.wait()
         result = dot(table_ref[...], jnp.concatenate(pieces, axis=0), ((1,), (1,)))
-        for tile in range(group * tiles):
-            out_ref[:, start * tiles + tile] = result[
-                :, tile * LANES : (tile + 1) * LANES
-            ].reshape(parts, sub, LANES)
+        for coil in range(coils):
+            for m, t in enumerate(members):
+                at = coil * rows + m * LANES
+                out_ref[:, coil * tiles + t] = result[:, at : at + LANES].reshape(parts, sub, LANES)
 
 
 def plane_kernel(
@@ -183,9 +197,7 @@
             (pick(c, p, 0) - pick(s, p, 1), pick(c, p, 1) + pick(s, p, 0)) for p in range(planes)
         ]
 
-    total = jnp.zeros((8, LANES), jnp.float32)
-    for start in range(0, coils, group):
-        members = range(start, start + group)
+    def enter(members):
         gathered = []
         for coil in members:
             for plane in range(planes):
@@ -198,8 +210,11 @@
                         )
                     )
                 gathered.append(jnp.concatenate(sides, axis=1))
-        after_x = dot(split_data(jnp.concatenate(gathered, axis=0), 1), xf_ref[...], ((1,), (0,)))
-        back = []
+        return dot(split_data(jnp.concatenate(gathered, axis=0), 1), xf_ref[...], ((1,), (0,)))
+
+    def forth(members, after_x):
+        total = jnp.zeros((8, LANES), jnp.float32)
+        out = []
         for n, coil in enumerate(members):
             at = [(n * planes + plane) * width_y for plane in range(planes)]
             even = forward(yfe_ref, jnp.concatenate([after_x[a : a + rows] for a in at], axis=1))
@@ -218,11 +233,20 @@
                     total = total + jnp.sum(square.reshape(rows // 8, 8, LANES), axis=0)
                     sums.append(low + high)
                     gaps.append(low - high)
-            even = backward(yie_ref, jnp.concatenate(sums, axis=1))
-            odd = backward(yio_ref, jnp.concatenate(gaps, axis=1))
+            out.append((jnp.concatenate(sums, axis=1), jnp.concatenate(gaps, axis=1)))
+        return out, total
+
+    def back_y(out):
+        back = []
+        for sums, gaps in out:
+            even = backward(yie_ref, sums)
+            odd = backward(yio_ref, gaps)
             for plane in range(planes):
                 back.append(jnp.concatenate(even[plane], axis=1))
                 back.append(jnp.concatenate(odd[plane], axis=1))
+        return back
+
+    def leave(members, back):
         returned = dot(split_data(jnp.concatenate(back, axis=0), 1), xi_ref[...], ((1,), (0,)))
         for n, coil in enumerate(members):
             for plane in range(planes):
@@ -232,6 +256,21 @@
                     first, second = interleave(block[:rows], block[rows:])
                     scatter(0, coil, 2 * plane + part, first)
                     scatter(1, coil, 2 * plane + part, second)
+
+    total = jnp.zeros((8, LANES), jnp.float32)
+    groups = [range(start, start + group) for start in range(0, coils, group)]
+    steps = range(len(groups))
+    held = {}
+    for n in range(len(groups) + 3):
+        if n in steps:
+            held[0, n] = enter(groups[n])
+        if n - 1 in steps:
+            held[1, n - 1], part_total = forth(groups[n - 1], held[0, n - 1])
+            total = total + part_total
+        if n - 2 in steps:
+            held[2, n - 2] = back_y(held[1, n - 2])
+        if n - 3 in steps:
+            leave(groups[n - 3], held[2, n - 3])
     out_ref[:, coils * tiles] = jnp.broadcast_to(total[None], (parts, sub, LANES))
 
 
@@ -243,7 +282,6 @@
     _, y_rows, x_rows, depth = image_ref.shape
     rows = y_rows * x_rows
     tiles = rows // LANES
-    present = present_ref[0].astype(jnp.float32)
     grad_re = jnp.zeros((rows, depth), jnp.float32)
     grad_im = jnp.zeros((rows, depth), jnp.float32)
     for coil in range(coils):
@@ -260,12 +298,34 @@
     shape = image_ref.shape[1:]
     moved_re = image_ref[0] - step_size * grad_re.reshape(shape)
     moved_im = image_ref[1] - step_size * grad_im.reshape(shape)
-    moved_ref[0] = moved_re
-    moved_ref[1] = moved_im
+    present = present_ref[0].astype(jnp.float32)
+    moved_ref[0] = present * moved_re
+    moved_ref[1] = present * moved_im
     energy = present * (moved_re * moved_re + moved_im * moved_im)
     energy_ref[: rows // 8] = energy.reshape(rows // 8, 8, depth)
     misfit = jnp.sum(in_ref[:, coils * tiles], axis=0)
     energy_ref[rows // 8] = jnp.full((8, depth), jnp.sum(misfit) * scale)
+
+
+def shrink_kernel(moved_ref, energy_ref, other_ref, image_hbm, misfit_ref, image_ref, sems):
+    parts, y_rows, x_rows, depth = moved_ref.shape
+    cut = y_rows // CHUNKS
+    count = cut * x_rows // 8
+    copies = []
+    for n in range(CHUNKS):
+        tiles, rows = pl.ds(n * count, count), pl.ds(n * cut, cut)
+        norm_value = jnp.sqrt((energy_ref[tiles] + other_ref[tiles]).reshape(cut, x_rows, depth))
+        factor = jnp.maximum(norm_value - threshold, 0.0) / jnp.maximum(norm_value, threshold)
+        for part in range(parts):
+            image_ref[part, rows] = moved_ref[part, rows] * factor
+        copies.append(
+            pltpu.make_async_copy(image_ref.at[:, rows], image_hbm.at[:, rows], sems.at[n])
+        )
+        copies[-1].start()
+    last = energy_ref.shape[0] - 1
+    misfit_ref[0, 0] = jnp.max(energy_ref[last] + other_ref[last])
+    for copy in copies:
+        copy.wait()
 
 
 def params():
@@ -305,21 +365,21 @@
     anywhere = pl.BlockSpec(memory_space=pl.ANY)
     local = pl.BlockSpec(memory_space=pltpu.VMEM)
     forward = pl.pallas_call(
-        functools.partial(z_forward_kernel, 2 if coils % 2 == 0 else 1),
+        functools.partial(z_forward_kernel, Z_CHUNK),
         out_shape=jax.ShapeDtypeStruct((parts, coils * tiles, sub, LANES), jnp.float32),
-        in_specs=[scalar, anywhere, anywhere, anywhere],
+        in_specs=[scalar] + [anywhere] * 3,
         out_specs=local,
         scratch_shapes=[
             pltpu.VMEM(pixels.shape, pixels.dtype),
             pltpu.VMEM(maps.shape, maps.dtype),
             pltpu.VMEM(zf.shape, zf.dtype),
-            pltpu.SemaphoreType.DMA((2 + coils,)),
+            pltpu.SemaphoreType.DMA((2 * pl.cdiv(tiles, Z_CHUNK) + 1,)),
         ],
         compiler_params=params(),
     )(available, in_hbm(pixels), in_hbm(maps), in_hbm(zf))
     received = lax.all_to_all(forward, ("pa", "pb"), split_axis=0, concat_axis=0, tiled=True)
     residual = pl.pallas_call(
-        functools.partial(plane_kernel, coils),
+        functools.partial(plane_kernel, 1),
         out_shape=jax.ShapeDtypeStruct((parts, coils * tiles + 1, sub, LANES), jnp.float32),
         in_specs=[scalar] + [local] * 9,
         out_specs=local,
@@ -352,13 +412,24 @@
             for low in range(shift, size + shift, 2):
                 first, second = low % size * pa + core, (low + 1) % size * pa + core
                 pairs += [(first, second), (second, first)]
-        energy = energy + lax.ppermute(energy, ("contrast", "pa"), pairs)
-    norm_value = jnp.sqrt(energy[:energy_tiles].reshape(y_rows, x_rows, depth))
-    present = available[0].astype(jnp.float32)
-    factor = jnp.maximum(norm_value - threshold, 0.0) / jnp.maximum(norm_value, threshold)
-    shrink = present * factor
-    result = jnp.transpose(moved * shrink[None], (0, 2, 1, 3))[None]
-    return (result, energy[energy_tiles, 0, 0])
+        other = lax.ppermute(energy, ("contrast", "pa"), pairs)
+        if step == 0:
+            energy = energy + other
+    result, misfit = pl.pallas_call(
+        shrink_kernel,
+        out_shape=(
+            jax.ShapeDtypeStruct(pixels.shape, jnp.float32),
+            jax.ShapeDtypeStruct((1, 1), jnp.float32),
+        ),
+        in_specs=[local] * 3,
+        out_specs=(anywhere, scalar),
+        scratch_shapes=[
+            pltpu.VMEM(pixels.shape, jnp.float32),
+            pltpu.SemaphoreType.DMA((CHUNKS,)),
+        ],
+        compiler_params=params(),
+    )(moved, energy, other)
+    return (jnp.transpose(result, (0, 2, 1, 3))[None], misfit[0, 0])
 
 
 def solution(mesh):

time: 113 us -> 111 us (0.982)
    pallas_call x2 -> x3, Pallas kernels: 10.3 us -> 10 us  [the longest x1 5.32 us: per_device(): pl.pallas_call(functools.partial(plane_kernel, 1), out_shape=jax.ShapeDty...]
where the time goes in v3:
time: 111 us; the launch traced here: 110 us
  blocking collectives  81.8 us (74%)
  Pallas kernels  11.5 us (10%)
  waiting for transfers between devices  11.2 us (10%)
  starting transfers between devices  4.41 us (4%)
  between operations  1.44 us (1%)
    all_to_all x1, blocking collectives, per_device(): lax.all_to_all(forward, ('pa', 'pb'), split_axis=0, concat_axis=0, tiled=...  42.8 us
    all_to_all x1, blocking collectives, per_device(): lax.all_to_all(residual, ('pa', 'pb'), split_axis=0, concat_axis=0, tiled...  39 us
    ppermute x2, waiting for transfers between devices, per_device(): other = lax.ppermute(energy, ('contrast', 'pa'), pairs)  11.2 us
    pallas_call x1, Pallas kernels, per_device(): pl.pallas_call(functools.partial(plane_kernel, 1), out_shape=jax.ShapeDty...  5.32 us
    ppermute x2, starting transfers between devices, per_device(): other = lax.ppermute(energy, ('contrast', 'pa'), pairs)  4.41 us
    pallas_call x1, Pallas kernels, per_device(): pl.pallas_call(functools.partial(z_forward_kernel, Z_CHUNK), out_shape=ja...  3.22 us
  transfers between devices with their start and end apart: 2, of which 2 were waited for; matrix products, arithmetic and copies ran while one was open for 0% of the time, Pallas kernels for 0%

profile of v3, /device:TPU:0, one launch (start us, length us, event | category | flops | bytes accessed | tf_op | source)
XLA Modules:
  0.0 110.5 jit_solution(639565104285800475)
XLA Ops:
  1.3 3.2 %shard_map.140 = f32[32,20,8,128]{3,2,1,0:T(8,128)S(1)} custom-call(s32[1]{0:T(128)S(6)} %copy.15.present_ref, f32[2,10,64,128]{3,2,1,0:T(8,128)} %bitcast.12, bf16[4,2,10,64,128]{4,3,2,1,0:T(8,128)(2,1)} %bitcast.10, bf16[256,768]{1,0:T(8,128)(2,1)} %constant.16.clone.table_hbm), custom_call_target="tpu_custom_call" | custom-call | tf_op jit(solution)/shard_map/pallas_call | solution.py:367
  4.5 0.0 copy-start.2
  4.5 0.0 copy-start.3
  4.5 0.0 copy-start.4
  4.5 0.0 copy-start.6
  4.6 0.0 copy-start.7
  4.6 0.0 copy-start.8
  4.6 0.0 copy-start.9
  4.6 0.0 copy-start.10
  4.6 42.8 %all_to_all.10.in_ref = f32[32,20,8,128]{3,2,1,0:T(8,128)S(1)} all-to-all(f32[32,20,8,128]{3,2,1,0:T(8,128)S(1)} %shard_map.140), channel_id=1, replica_groups=mesh['contrast'=4,'pa'=2,'pb'=16] {'pa','pb'}, dimensions={0} | all-to-all | bytes 5242880 | tf_op jit(solution)/shard_map/all_to_all | solution.py:380
  47.4 0.0 copy-done.2
  47.4 0.0 copy-done.3
  47.4 0.0 copy-done.4
  47.4 0.0 copy-done.6
  47.4 0.0 copy-done.7
  47.4 0.0 copy-done.8
  47.4 0.0 copy-done.9
  47.4 0.0 copy-done.10
  47.5 5.3 %shard_map.141 = f32[32,21,8,128]{3,2,1,0:T(8,128)S(1)} custom-call(s32[1]{0:T(128)S(6)} %copy.15.present_ref, f32[32,20,8,128]{3,2,1,0:T(8,128)S(1)} %all_to_all.10.in_ref, bf16[768,256]{1,0:T(8,128)(2,1)S(1)} %copy-done.4, bf16[768,256]{1,0:T(8,128)(2,1)S(1)} %copy-done.3, bf16[4,2,4,160,128]{4,3,2,1,0:T(8,128)(2,1)S(1)} %bitcast.14, ...), custom_call_target="tpu_custom_call" | custom-call | tf_op jit(solution)/shard_map/pallas_call | solution.py:381
  52.8 0.0 copy-start
  52.8 0.0 copy-start.1
  52.8 0.0 copy-start.5
  52.8 39.0 %all_to_all.11.in_ref = f32[32,21,8,128]{3,2,1,0:T(8,128)S(1)} all-to-all(f32[32,21,8,128]{3,2,1,0:T(8,128)S(1)} %shard_map.141), channel_id=1, replica_groups=mesh['contrast'=4,'pa'=2,'pb'=16] {'pa','pb'}, dimensions={0} | all-to-all | bytes 5505024 | tf_op jit(solution)/shard_map/all_to_all | solution.py:391
  91.9 0.0 copy-done
  91.9 0.0 copy-done.1
  91.9 0.0 copy-done.5
  91.9 1.5 %shard_map.142 = (f32[2,10,64,128]{3,2,1,0:T(8,128)S(1)}, f32[81,8,128]{2,1,0:T(8,128)S(1)}) custom-call(s32[1]{0:T(128)S(6)} %copy.15.present_ref, f32[32,21,8,128]{3,2,1,0:T(8,128)S(1)} %all_to_all.11.in_ref, bf16[4,2,10,64,128]{4,3,2,1,0:T(8,128)(2,1)S(1)} %bitcast.11, f32[2,10,64,128]{3,2,1,0:T(8,128)S(1)} %bitcast.13, bf16[768,256]{1,0:T(8,128)(2,1)S(1)} %copy-done.5), custom_call_target="tpu_custom_call" | custom-call | tf_op jit(solution)/shard_map/pallas_call | solution.py:396
  93.3 1.6 %collective-permute-start = (f32[81,8,128]{2,1,0:T(8,128)S(1)}, f32[81,8,128]{2,1,0:T(8,128)S(1)}, u32[]{:S(2)}, u32[]{:S(2)}) collective-permute-start(f32[81,8,128]{2,1,0:T(8,128)S(1)} %get-tuple-element.7), channel_id=1, source_target_pairs={{0,32},{32,0},{64,96},{96,64},{48,80},{80,48},{112,16},{16,112},{1... | collective-permute-start | bytes 995336 | tf_op jit(solution)/shard_map/ppermute | solution.py:415
  94.9 5.6 %collective-permute-done = f32[81,8,128]{2,1,0:T(8,128)S(1)} collective-permute-done((f32[81,8,128]{2,1,0:T(8,128)S(1)}, f32[81,8,128]{2,1,0:T(8,128)S(1)}, u32[]{:S(2)}, u32[]{:S(2)}) %collective-permute-start) | collective-permute-done | bytes 331808 | tf_op jit(solution)/shard_map/ppermute | solution.py:415
  100.6 2.8 %collective-permute-start.1 = (f32[81,8,128]{2,1,0:T(8,128)S(1)}, f32[81,8,128]{2,1,0:T(8,128)S(1)}, u32[]{:S(2)}, u32[]{:S(2)}) collective-permute-start(f32[81,8,128]{2,1,0:T(8,128)S(1)} %add.3.energy_ref), channel_id=1, source_target_pairs={{32,64},{64,32},{96,0},{0,96},{16,48},{48,16},{80,112},{112,80},{3... | collective-permute-start | bytes 995336 | tf_op jit(solution)/shard_map/ppermute | solution.py:415
  103.4 5.6 %collective-permute-done.1.other_ref = f32[81,8,128]{2,1,0:T(8,128)S(1)} collective-permute-done((f32[81,8,128]{2,1,0:T(8,128)S(1)}, f32[81,8,128]{2,1,0:T(8,128)S(1)}, u32[]{:S(2)}, u32[]{:S(2)}) %collective-permute-start.1) | collective-permute-done | bytes 331808 | tf_op jit(solution)/shard_map/ppermute | solution.py:415
  109.0 1.5 %shard_map.143 = (f32[2,10,64,128]{3,2,1,0:T(8,128)}, f32[1,1]{1,0:T(1,128)}) custom-call(f32[2,10,64,128]{3,2,1,0:T(8,128)S(1)} %get-tuple-element.6.moved_ref, f32[81,8,128]{2,1,0:T(8,128)S(1)} %add.3.energy_ref, f32[81,8,128]{2,1,0:T(8,128)S(1)} %collective-permute-done.1.other_ref), custom_call_target="tpu_custom_call" | custom-call | tf_op jit(solution)/shard_map/pallas_call | solution.py:418
  (1 shorter events, 0.0 us)
Async XLA Ops:
  4.5 42.9 %copy-start.2 = (bf16[1,4,2,4,160,128]{5,4,3,2,1,0:T(8,128)(2,1)S(1)}, bf16[1,4,2,4,160,128]{5,4,3,2,1,0:T(8,128)(2,1)}, u32[]{:S(2)}) copy-start(bf16[1,4,2,4,160,128]{5,4,3,2,1,0:T(8,128)(2,1)} %param.15) | copy-start | bytes 3932164
  4.5 42.9 %copy-start.3 = (bf16[768,256]{1,0:T(8,128)(2,1)S(1)}, bf16[768,256]{1,0:T(8,128)(2,1)}, u32[]{:S(2)}) copy-start(bf16[768,256]{1,0:T(8,128)(2,1)} %constant.19.clone.xi_ref) | copy-start | bytes 1179652
  4.5 42.9 %copy-start.4 = (bf16[768,256]{1,0:T(8,128)(2,1)S(1)}, bf16[768,256]{1,0:T(8,128)(2,1)}, u32[]{:S(2)}) copy-start(bf16[768,256]{1,0:T(8,128)(2,1)} %constant.18.clone.xf_ref) | copy-start | bytes 1179652
  4.5 42.9 %copy-start.6 = (s32[1,4,160,128]{3,2,1,0:T(8,128)S(1)}, s32[1,4,160,128]{3,2,1,0:T(8,128)}, u32[]{:S(2)}) copy-start(s32[1,4,160,128]{3,2,1,0:T(8,128)} %param.16) | copy-start | bytes 983044
  4.6 42.9 %copy-start.7 = (bf16[160,240]{1,0:T(8,128)(2,1)S(1)}, bf16[160,240]{1,0:T(8,128)(2,1)}, u32[]{:S(2)}) copy-start(bf16[160,240]{1,0:T(8,128)(2,1)} %constant.23.clone.yio_ref) | copy-start | bytes 230404
  4.6 42.9 %copy-start.8 = (bf16[160,240]{1,0:T(8,128)(2,1)S(1)}, bf16[160,240]{1,0:T(8,128)(2,1)}, u32[]{:S(2)}) copy-start(bf16[160,240]{1,0:T(8,128)(2,1)} %constant.22.clone.yfo_ref) | copy-start | bytes 230404
  4.6 42.9 %copy-start.9 = (bf16[160,240]{1,0:T(8,128)(2,1)S(1)}, bf16[160,240]{1,0:T(8,128)(2,1)}, u32[]{:S(2)}) copy-start(bf16[160,240]{1,0:T(8,128)(2,1)} %constant.21.clone.yie_ref) | copy-start | bytes 230404
  4.6 42.9 %copy-start.10 = (bf16[160,240]{1,0:T(8,128)(2,1)S(1)}, bf16[160,240]{1,0:T(8,128)(2,1)}, u32[]{:S(2)}) copy-start(bf16[160,240]{1,0:T(8,128)(2,1)} %constant.20.clone.yfe_ref) | copy-start | bytes 230404
  52.8 39.1 %copy-start = (bf16[4,2,64,10,128]{4,2,3,1,0:T(8,128)(2,1)S(1)}, bf16[4,2,64,10,128]{4,2,3,1,0:T(8,128)(2,1)}, u32[]{:S(2)}) copy-start(bf16[4,2,64,10,128]{4,2,3,1,0:T(8,128)(2,1)} %param.14) | copy-start | bytes 3932164
  52.8 39.1 %copy-start.1 = (f32[1,2,64,10,128]{4,2,3,1,0:T(8,128)S(1)}, f32[1,2,64,10,128]{4,2,3,1,0:T(8,128)}, u32[]{:S(2)}) copy-start(f32[1,2,64,10,128]{4,2,3,1,0:T(8,128)} %param.13) | copy-start | bytes 1966084
  52.8 39.1 %copy-start.5 = (bf16[768,256]{1,0:T(8,128)(2,1)S(1)}, bf16[768,256]{1,0:T(8,128)(2,1)}, u32[]{:S(2)}) copy-start(bf16[768,256]{1,0:T(8,128)(2,1)} %constant.17.clone.table_ref) | copy-start | bytes 1179652
  93.3 7.2 %collective-permute-start = (f32[81,8,128]{2,1,0:T(8,128)S(1)}, f32[81,8,128]{2,1,0:T(8,128)S(1)}, u32[]{:S(2)}, u32[]{:S(2)}) collective-permute-start(f32[81,8,128]{2,1,0:T(8,128)S(1)} %get-tuple-element.7), channel_id=1, source_target_pairs={{0,32},{32,0},{64,96},{96,64},{48,80},{80,48},{112,16},{16,112},{1... | collective-permute-start | bytes 995336 | tf_op jit(solution)/shard_map/ppermute | solution.py:415
  100.6 8.4 %collective-permute-start.1 = (f32[81,8,128]{2,1,0:T(8,128)S(1)}, f32[81,8,128]{2,1,0:T(8,128)S(1)}, u32[]{:S(2)}, u32[]{:S(2)}) collective-permute-start(f32[81,8,128]{2,1,0:T(8,128)S(1)} %add.3.energy_ref), channel_id=1, source_target_pairs={{32,64},{64,32},{96,0},{0,96},{16,48},{48,16},{80,112},{112,80},{3... | collective-permute-start | bytes 995336 | tf_op jit(solution)/shard_map/ppermute | solution.py:415

commit v4 on v3

--- a/solution.py
+++ b/solution.py
@@ -275,7 +275,7 @@
 
 
 def z_inverse_kernel(
-    scale, present_ref, in_ref, maps_ref, image_ref, table_ref, moved_ref, energy_ref
+    scale, present_ref, in_ref, maps_ref, image_ref, table_ref, moved_ref, *energy_refs
 ):
     parts, _, sub, _ = in_ref.shape
     coils = maps_ref.shape[0]
@@ -302,19 +302,26 @@
     moved_ref[0] = present * moved_re
     moved_ref[1] = present * moved_im
     energy = present * (moved_re * moved_re + moved_im * moved_im)
-    energy_ref[: rows // 8] = energy.reshape(rows // 8, 8, depth)
+    energy = energy.reshape(rows // 8, 8, depth)
+    cut = rows // 8 // len(energy_refs)
+    for n, energy_ref in enumerate(energy_refs):
+        energy_ref[:cut] = energy[n * cut : (n + 1) * cut]
     misfit = jnp.sum(in_ref[:, coils * tiles], axis=0)
-    energy_ref[rows // 8] = jnp.full((8, depth), jnp.sum(misfit) * scale)
-
-
-def shrink_kernel(moved_ref, energy_ref, other_ref, image_hbm, misfit_ref, image_ref, sems):
+    energy_refs[0][cut] = jnp.full((8, depth), jnp.sum(misfit) * scale)
+
+
+def shrink_kernel(*refs):
+    moved_ref = refs[0]
+    energy_refs, other_refs = refs[1 : 1 + CHUNKS], refs[1 + CHUNKS : 1 + 2 * CHUNKS]
+    image_hbm, misfit_ref, image_ref, sems = refs[1 + 2 * CHUNKS :]
     parts, y_rows, x_rows, depth = moved_ref.shape
     cut = y_rows // CHUNKS
     count = cut * x_rows // 8
     copies = []
     for n in range(CHUNKS):
-        tiles, rows = pl.ds(n * count, count), pl.ds(n * cut, cut)
-        norm_value = jnp.sqrt((energy_ref[tiles] + other_ref[tiles]).reshape(cut, x_rows, depth))
+        rows = pl.ds(n * cut, cut)
+        energy = energy_refs[n][:count] + other_refs[n][:count]
+        norm_value = jnp.sqrt(energy.reshape(cut, x_rows, depth))
         factor = jnp.maximum(norm_value - threshold, 0.0) / jnp.maximum(norm_value, threshold)
         for part in range(parts):
             image_ref[part, rows] = moved_ref[part, rows] * factor
@@ -322,8 +329,7 @@
             pltpu.make_async_copy(image_ref.at[:, rows], image_hbm.at[:, rows], sems.at[n])
         )
         copies[-1].start()
-    last = energy_ref.shape[0] - 1
-    misfit_ref[0, 0] = jnp.max(energy_ref[last] + other_ref[last])
+    misfit_ref[0, 0] = jnp.max(energy_refs[0][count] + other_refs[0][count])
     for copy in copies:
         copy.wait()
 
@@ -392,43 +398,48 @@
 
     contrasts = lax.axis_size("contrast") * image.shape[0]
     scale = 1.0 / (2.0 * contrasts * coils * width_x * width_y * depth)
-    energy_tiles = y_rows * x_rows // 8
-    moved, energy = pl.pallas_call(
+    energy_tiles = y_rows * x_rows // 8 // CHUNKS
+    moved, *energies = pl.pallas_call(
         functools.partial(z_inverse_kernel, scale),
         out_shape=(
             jax.ShapeDtypeStruct(pixels.shape, jnp.float32),
-            jax.ShapeDtypeStruct((energy_tiles + 1, 8, depth), jnp.float32),
+            *[
+                jax.ShapeDtypeStruct((energy_tiles + (n == 0), 8, depth), jnp.float32)
+                for n in range(CHUNKS)
+            ],
         ),
         in_specs=[scalar] + [local] * 4,
-        out_specs=(local, local),
+        out_specs=(local,) * (1 + CHUNKS),
         compiler_params=params(),
     )(available, returned, maps, pixels, zi)
 
     size = lax.axis_size("contrast")
-    for step in range(2):
+
+    def other_sum(value, turn):
         pairs = []
         for core in range(pa):
-            shift = (core + step) % 2
+            shift = (core + turn) % 2
             for low in range(shift, size + shift, 2):
                 first, second = low % size * pa + core, (low + 1) % size * pa + core
                 pairs += [(first, second), (second, first)]
-        other = lax.ppermute(energy, ("contrast", "pa"), pairs)
-        if step == 0:
-            energy = energy + other
+        return lax.ppermute(value, ("contrast", "pa"), pairs)
+
+    energies = [value + other_sum(value, n) for n, value in enumerate(energies)]
+    others = [other_sum(value, n + 1) for n, value in enumerate(energies)]
     result, misfit = pl.pallas_call(
         shrink_kernel,
         out_shape=(
             jax.ShapeDtypeStruct(pixels.shape, jnp.float32),
             jax.ShapeDtypeStruct((1, 1), jnp.float32),
         ),
-        in_specs=[local] * 3,
+        in_specs=[local] * (1 + 2 * CHUNKS),
         out_specs=(anywhere, scalar),
         scratch_shapes=[
             pltpu.VMEM(pixels.shape, jnp.float32),
             pltpu.SemaphoreType.DMA((CHUNKS,)),
         ],
         compiler_params=params(),
-    )(moved, energy, other)
+    )(moved, *energies, *others)
     return (jnp.transpose(result, (0, 2, 1, 3))[None], misfit[0, 0])
 
 

time: 111 us -> 111 us (level)
  waiting for transfers between devices: 11.2 us -> 8.72 us
  starting transfers between devices: 4.41 us -> 6 us
    ppermute x2 -> x4, waiting for transfers between devices: 11.2 us -> 8.72 us  [other_sum(): return lax.ppermute(value, ('contrast', 'pa'), pairs)]
    ppermute x2 -> x4, starting transfers between devices: 4.41 us -> 6 us  [other_sum(): return lax.ppermute(value, ('contrast', 'pa'), pairs)]
  transfers between devices with their start and end apart: 2 -> 4, of which waited for: 2 -> 3; matrix products, arithmetic and copies ran while one was open for 0% -> 0% of each run, Pallas kernels for 0% -> 0%
where the time goes in v4:
time: 111 us; the launch traced here: 110 us
  blocking collectives  81.8 us (74%)
  Pallas kernels  11.5 us (10%)
  waiting for transfers between devices  8.72 us (8%)
  starting transfers between devices  6 us (5%)
  between operations  1.45 us (1%)
    all_to_all x1, blocking collectives, per_device(): lax.all_to_all(forward, ('pa', 'pb'), split_axis=0, concat_axis=0, tiled=...  42.8 us
    all_to_all x1, blocking collectives, per_device(): lax.all_to_all(residual, ('pa', 'pb'), split_axis=0, concat_axis=0, tiled...  39 us
    ppermute x4, waiting for transfers between devices, other_sum(): return lax.ppermute(value, ('contrast', 'pa'), pairs)  8.72 us
    ppermute x4, starting transfers between devices, other_sum(): return lax.ppermute(value, ('contrast', 'pa'), pairs)  6 us
    pallas_call x1, Pallas kernels, per_device(): pl.pallas_call(functools.partial(plane_kernel, 1), out_shape=jax.ShapeDty...  5.32 us
    pallas_call x1, Pallas kernels, per_device(): pl.pallas_call(functools.partial(z_forward_kernel, Z_CHUNK), out_shape=ja...  3.22 us
  transfers between devices with their start and end apart: 4, of which 3 were waited for; matrix products, arithmetic and copies ran while one was open for 0% of the time, Pallas kernels for 0%

profile of v4, /device:TPU:0, one launch (start us, length us, event | category | flops | bytes accessed | tf_op | source)
XLA Modules:
  0.0 109.6 jit_solution(17291103814902556811)
XLA Ops:
  1.3 3.2 %shard_map.140 = f32[32,20,8,128]{3,2,1,0:T(8,128)S(1)} custom-call(s32[1]{0:T(128)S(6)} %copy.15.present_ref, f32[2,10,64,128]{3,2,1,0:T(8,128)} %bitcast.12, bf16[4,2,10,64,128]{4,3,2,1,0:T(8,128)(2,1)} %bitcast.10, bf16[256,768]{1,0:T(8,128)(2,1)} %constant.16.clone.table_hbm), custom_call_target="tpu_custom_call" | custom-call | tf_op jit(solution)/shard_map/pallas_call | solution.py:373
  4.5 0.0 copy-start.2
  4.5 0.0 copy-start.3
  4.5 0.0 copy-start.4
  4.5 0.0 copy-start.6
  4.6 0.0 copy-start.7
  4.6 0.0 copy-start.8
  4.6 0.0 copy-start.9
  4.6 0.0 copy-start.10
  4.6 42.8 %all_to_all.10.in_ref = f32[32,20,8,128]{3,2,1,0:T(8,128)S(1)} all-to-all(f32[32,20,8,128]{3,2,1,0:T(8,128)S(1)} %shard_map.140), channel_id=1, replica_groups=mesh['contrast'=4,'pa'=2,'pb'=16] {'pa','pb'}, dimensions={0} | all-to-all | bytes 5242880 | tf_op jit(solution)/shard_map/all_to_all | solution.py:386
  47.4 0.0 copy-done.2
  47.4 0.0 copy-done.3
  47.4 0.0 copy-done.4
  47.4 0.0 copy-done.6
  47.4 0.0 copy-done.7
  47.4 0.0 copy-done.8
  47.4 0.0 copy-done.9
  47.4 0.0 copy-done.10
  47.5 5.3 %shard_map.141 = f32[32,21,8,128]{3,2,1,0:T(8,128)S(1)} custom-call(s32[1]{0:T(128)S(6)} %copy.15.present_ref, f32[32,20,8,128]{3,2,1,0:T(8,128)S(1)} %all_to_all.10.in_ref, bf16[768,256]{1,0:T(8,128)(2,1)S(1)} %copy-done.4, bf16[768,256]{1,0:T(8,128)(2,1)S(1)} %copy-done.3, bf16[4,2,4,160,128]{4,3,2,1,0:T(8,128)(2,1)S(1)} %bitcast.14, ...), custom_call_target="tpu_custom_call" | custom-call | tf_op jit(solution)/shard_map/pallas_call | solution.py:387
  52.8 0.0 copy-start
  52.8 0.0 copy-start.1
  52.8 0.0 copy-start.5
  52.8 39.0 %all_to_all.11.in_ref = f32[32,21,8,128]{3,2,1,0:T(8,128)S(1)} all-to-all(f32[32,21,8,128]{3,2,1,0:T(8,128)S(1)} %shard_map.141), channel_id=1, replica_groups=mesh['contrast'=4,'pa'=2,'pb'=16] {'pa','pb'}, dimensions={0} | all-to-all | bytes 5505024 | tf_op jit(solution)/shard_map/all_to_all | solution.py:397
  91.9 0.0 copy-done
  91.9 0.0 copy-done.1
  91.9 0.0 copy-done.5
  91.9 1.5 %shard_map.142 = (f32[2,10,64,128]{3,2,1,0:T(8,128)S(1)}, f32[41,8,128]{2,1,0:T(8,128)S(1)}, f32[40,8,128]{2,1,0:T(8,128)S(1)}) custom-call(s32[1]{0:T(128)S(6)} %copy.15.present_ref, f32[32,21,8,128]{3,2,1,0:T(8,128)S(1)} %all_to_all.11.in_ref, bf16[4,2,10,64,128]{4,3,2,1,0:T(8,128)(2,1)S(1)} %bitcast.11, f32[2,10,64,128]{3,2,1,0:T(8,128)S(1)} %bitcast.13, ...), custom_call_target="tpu_custom_call" | custom-call | tf_op jit(solution)/shard_map/pallas_call | solution.py:402
  93.3 1.6 %collective-permute-start = (f32[41,8,128]{2,1,0:T(8,128)S(1)}, f32[41,8,128]{2,1,0:T(8,128)S(1)}, u32[]{:S(2)}, u32[]{:S(2)}) collective-permute-start(f32[41,8,128]{2,1,0:T(8,128)S(1)} %get-tuple-element.8), channel_id=1, source_target_pairs={{0,32},{32,0},{64,96},{96,64},{48,80},{80,48},{112,16},{16,112},{1... | collective-permute-start | bytes 503816 | tf_op jit(solution)/shard_map/ppermute | solution.py:425
  94.9 2.1 %collective-permute-start.1 = (f32[40,8,128]{2,1,0:T(8,128)S(1)}, f32[40,8,128]{2,1,0:T(8,128)S(1)}, u32[]{:S(2)}, u32[]{:S(2)}) collective-permute-start(f32[40,8,128]{2,1,0:T(8,128)S(1)} %get-tuple-element.9), channel_id=1, source_target_pairs={{32,64},{64,32},{96,0},{0,96},{16,48},{48,16},{80,112},{112,80},{3... | collective-permute-start | bytes 491528 | tf_op jit(solution)/shard_map/ppermute | solution.py:425
  97.0 2.9 %collective-permute-done = f32[41,8,128]{2,1,0:T(8,128)S(1)} collective-permute-done((f32[41,8,128]{2,1,0:T(8,128)S(1)}, f32[41,8,128]{2,1,0:T(8,128)S(1)}, u32[]{:S(2)}, u32[]{:S(2)}) %collective-permute-start) | collective-permute-done | bytes 167968 | tf_op jit(solution)/shard_map/ppermute | solution.py:425
  99.9 2.0 %collective-permute-start.2 = (f32[41,8,128]{2,1,0:T(8,128)S(1)}, f32[41,8,128]{2,1,0:T(8,128)S(1)}, u32[]{:S(2)}, u32[]{:S(2)}) collective-permute-start(f32[41,8,128]{2,1,0:T(8,128)S(1)} %add.6.refs_1_), channel_id=1, source_target_pairs={{32,64},{64,32},{96,0},{0,96},{16,48},{48,16},{80,112},{112,80},{3... | collective-permute-start | bytes 503816 | tf_op jit(solution)/shard_map/ppermute | solution.py:425
  101.9 0.0 collective-permute-done.1
  101.9 0.4 collective-permute-start.3
  102.2 5.0 %collective-permute-done.3.refs_4_ = f32[40,8,128]{2,1,0:T(8,128)S(1)} collective-permute-done((f32[40,8,128]{2,1,0:T(8,128)S(1)}, f32[40,8,128]{2,1,0:T(8,128)S(1)}, u32[]{:S(2)}, u32[]{:S(2)}) %collective-permute-start.3) | collective-permute-done | bytes 163872 | tf_op jit(solution)/shard_map/ppermute | solution.py:425
  107.3 0.8 collective-permute-done.2.refs_3_
  108.1 1.5 %shard_map.143 = (f32[2,10,64,128]{3,2,1,0:T(8,128)}, f32[1,1]{1,0:T(1,128)}) custom-call(f32[2,10,64,128]{3,2,1,0:T(8,128)S(1)} %get-tuple-element.7.refs_0_, f32[41,8,128]{2,1,0:T(8,128)S(1)} %add.6.refs_1_, f32[40,8,128]{2,1,0:T(8,128)S(1)} %add.7.refs_2_, f32[41,8,128]{2,1,0:T(8,128)S(1)} %collective-permute-done.2.refs_3_, ...), custom_call_target="tpu_custom_call" | custom-call | tf_op jit(solution)/shard_map/pallas_call | solution.py:429
  (2 shorter events, 0.0 us)
Async XLA Ops:
  4.5 42.9 %copy-start.2 = (bf16[1,4,2,4,160,128]{5,4,3,2,1,0:T(8,128)(2,1)S(1)}, bf16[1,4,2,4,160,128]{5,4,3,2,1,0:T(8,128)(2,1)}, u32[]{:S(2)}) copy-start(bf16[1,4,2,4,160,128]{5,4,3,2,1,0:T(8,128)(2,1)} %param.15) | copy-start | bytes 3932164
  4.5 42.9 %copy-start.3 = (bf16[768,256]{1,0:T(8,128)(2,1)S(1)}, bf16[768,256]{1,0:T(8,128)(2,1)}, u32[]{:S(2)}) copy-start(bf16[768,256]{1,0:T(8,128)(2,1)} %constant.19.clone.xi_ref) | copy-start | bytes 1179652
  4.5 42.9 %copy-start.4 = (bf16[768,256]{1,0:T(8,128)(2,1)S(1)}, bf16[768,256]{1,0:T(8,128)(2,1)}, u32[]{:S(2)}) copy-start(bf16[768,256]{1,0:T(8,128)(2,1)} %constant.18.clone.xf_ref) | copy-start | bytes 1179652
  4.5 42.9 %copy-start.6 = (s32[1,4,160,128]{3,2,1,0:T(8,128)S(1)}, s32[1,4,160,128]{3,2,1,0:T(8,128)}, u32[]{:S(2)}) copy-start(s32[1,4,160,128]{3,2,1,0:T(8,128)} %param.16) | copy-start | bytes 983044
  4.6 42.9 %copy-start.7 = (bf16[160,240]{1,0:T(8,128)(2,1)S(1)}, bf16[160,240]{1,0:T(8,128)(2,1)}, u32[]{:S(2)}) copy-start(bf16[160,240]{1,0:T(8,128)(2,1)} %constant.23.clone.yio_ref) | copy-start | bytes 230404
  4.6 42.9 %copy-start.8 = (bf16[160,240]{1,0:T(8,128)(2,1)S(1)}, bf16[160,240]{1,0:T(8,128)(2,1)}, u32[]{:S(2)}) copy-start(bf16[160,240]{1,0:T(8,128)(2,1)} %constant.22.clone.yfo_ref) | copy-start | bytes 230404
  4.6 42.9 %copy-start.9 = (bf16[160,240]{1,0:T(8,128)(2,1)S(1)}, bf16[160,240]{1,0:T(8,128)(2,1)}, u32[]{:S(2)}) copy-start(bf16[160,240]{1,0:T(8,128)(2,1)} %constant.21.clone.yie_ref) | copy-start | bytes 230404
  4.6 42.9 %copy-start.10 = (bf16[160,240]{1,0:T(8,128)(2,1)S(1)}, bf16[160,240]{1,0:T(8,128)(2,1)}, u32[]{:S(2)}) copy-start(bf16[160,240]{1,0:T(8,128)(2,1)} %constant.20.clone.yfe_ref) | copy-start | bytes 230404
  52.8 39.1 %copy-start = (bf16[4,2,64,10,128]{4,2,3,1,0:T(8,128)(2,1)S(1)}, bf16[4,2,64,10,128]{4,2,3,1,0:T(8,128)(2,1)}, u32[]{:S(2)}) copy-start(bf16[4,2,64,10,128]{4,2,3,1,0:T(8,128)(2,1)} %param.14) | copy-start | bytes 3932164
  52.8 39.1 %copy-start.1 = (f32[1,2,64,10,128]{4,2,3,1,0:T(8,128)S(1)}, f32[1,2,64,10,128]{4,2,3,1,0:T(8,128)}, u32[]{:S(2)}) copy-start(f32[1,2,64,10,128]{4,2,3,1,0:T(8,128)} %param.13) | copy-start | bytes 1966084
  52.8 39.1 %copy-start.5 = (bf16[768,256]{1,0:T(8,128)(2,1)S(1)}, bf16[768,256]{1,0:T(8,128)(2,1)}, u32[]{:S(2)}) copy-start(bf16[768,256]{1,0:T(8,128)(2,1)} %constant.17.clone.table_ref) | copy-start | bytes 1179652
  93.3 6.5 %collective-permute-start = (f32[41,8,128]{2,1,0:T(8,128)S(1)}, f32[41,8,128]{2,1,0:T(8,128)S(1)}, u32[]{:S(2)}, u32[]{:S(2)}) collective-permute-start(f32[41,8,128]{2,1,0:T(8,128)S(1)} %get-tuple-element.8), channel_id=1, source_target_pairs={{0,32},{32,0},{64,96},{96,64},{48,80},{80,48},{112,16},{16,112},{1... | collective-permute-start | bytes 503816 | tf_op jit(solution)/shard_map/ppermute | solution.py:425
  94.9 7.0 %collective-permute-start.1 = (f32[40,8,128]{2,1,0:T(8,128)S(1)}, f32[40,8,128]{2,1,0:T(8,128)S(1)}, u32[]{:S(2)}, u32[]{:S(2)}) collective-permute-start(f32[40,8,128]{2,1,0:T(8,128)S(1)} %get-tuple-element.9), channel_id=1, source_target_pairs={{32,64},{64,32},{96,0},{0,96},{16,48},{48,16},{80,112},{112,80},{3... | collective-permute-start | bytes 491528 | tf_op jit(solution)/shard_map/ppermute | solution.py:425
  99.9 8.2 %collective-permute-start.2 = (f32[41,8,128]{2,1,0:T(8,128)S(1)}, f32[41,8,128]{2,1,0:T(8,128)S(1)}, u32[]{:S(2)}, u32[]{:S(2)}) collective-permute-start(f32[41,8,128]{2,1,0:T(8,128)S(1)} %add.6.refs_1_), channel_id=1, source_target_pairs={{32,64},{64,32},{96,0},{0,96},{16,48},{48,16},{80,112},{112,80},{3... | collective-permute-start | bytes 503816 | tf_op jit(solution)/shard_map/ppermute | solution.py:425
  101.9 5.4 %collective-permute-start.3 = (f32[40,8,128]{2,1,0:T(8,128)S(1)}, f32[40,8,128]{2,1,0:T(8,128)S(1)}, u32[]{:S(2)}, u32[]{:S(2)}) collective-permute-start(f32[40,8,128]{2,1,0:T(8,128)S(1)} %add.7.refs_2_), channel_id=1, source_target_pairs={{0,32},{32,0},{64,96},{96,64},{48,80},{80,48},{112,16},{16,112},{1... | collective-permute-start | bytes 491528 | tf_op jit(solution)/shard_map/ppermute | solution.py:425

commit v5 on v4

--- a/solution.py
+++ b/solution.py
@@ -14,7 +14,6 @@
 threshold = 2.5
 LANES = 128
 CHUNKS = 2
-Z_CHUNK = 2
 VMEM_LIMIT = 40 * 1024 * 1024
 
 
@@ -86,7 +85,7 @@
 
 
 def z_forward_kernel(
-    chunk, present_ref, image_hbm, maps_hbm, table_hbm, out_ref, image_ref, maps_ref, table_ref, sems
+    first, present_ref, image_hbm, maps_hbm, table_hbm, out_ref, image_ref, maps_ref, table_ref, sems
 ):
     coils = maps_ref.shape[0]
     _, y_rows, x_rows, depth = image_ref.shape
@@ -95,8 +94,9 @@
     tiles = y_rows // pair
     table_copy = pltpu.make_async_copy(table_hbm, table_ref, sems.at[0])
     copies = []
-    for t in range(0, tiles, chunk):
-        along = pl.ds(t * pair, min(chunk, tiles - t) * pair)
+    spans = [range(0, first), range(first, tiles)]
+    for span in spans:
+        along = pl.ds(span.start * pair, len(span) * pair)
         n = len(copies)
         copies.append(
             [
@@ -116,7 +116,7 @@
     for n, both in enumerate(copies):
         for copy in both:
             copy.wait()
-        members = range(n * chunk, min((n + 1) * chunk, tiles))
+        members = spans[n]
         along = pl.ds(members.start * pair, len(members) * pair)
         rows = len(members) * LANES
         image_re = image_ref[0, along].reshape(rows, depth)
@@ -371,7 +371,7 @@
     anywhere = pl.BlockSpec(memory_space=pl.ANY)
     local = pl.BlockSpec(memory_space=pltpu.VMEM)
     forward = pl.pallas_call(
-        functools.partial(z_forward_kernel, Z_CHUNK),
+        functools.partial(z_forward_kernel, 1),
         out_shape=jax.ShapeDtypeStruct((parts, coils * tiles, sub, LANES), jnp.float32),
         in_specs=[scalar] + [anywhere] * 3,
         out_specs=local,
@@ -379,7 +379,7 @@
             pltpu.VMEM(pixels.shape, pixels.dtype),
             pltpu.VMEM(maps.shape, maps.dtype),
             pltpu.VMEM(zf.shape, zf.dtype),
-            pltpu.SemaphoreType.DMA((2 * pl.cdiv(tiles, Z_CHUNK) + 1,)),
+            pltpu.SemaphoreType.DMA((5,)),
         ],
         compiler_params=params(),
     )(available, in_hbm(pixels), in_hbm(maps), in_hbm(zf))

time: 111 us -> 110 us (level)
  no operation moved by 1% of the time
where the time goes in v5:
time: 110 us; the launch traced here: 109 us
  blocking collectives  81.8 us (74%)
  Pallas kernels  11 us (10%)
  waiting for transfers between devices  8.72 us (8%)
  starting transfers between devices  6.01 us (5%)
  between operations  1.45 us (1%)
    all_to_all x1, blocking collectives, per_device(): lax.all_to_all(forward, ('pa', 'pb'), split_axis=0, concat_axis=0, tiled=...  42.8 us
    all_to_all x1, blocking collectives, per_device(): lax.all_to_all(residual, ('pa', 'pb'), split_axis=0, concat_axis=0, tiled...  39 us
    ppermute x4, waiting for transfers between devices, other_sum(): return lax.ppermute(value, ('contrast', 'pa'), pairs)  8.72 us
    ppermute x4, starting transfers between devices, other_sum(): return lax.ppermute(value, ('contrast', 'pa'), pairs)  6.01 us
    pallas_call x1, Pallas kernels, per_device(): pl.pallas_call(functools.partial(plane_kernel, 1), out_shape=jax.ShapeDty...  5.32 us
    pallas_call x1, Pallas kernels, per_device(): pl.pallas_call(functools.partial(z_forward_kernel, 1), out_shape=jax.Shap...  2.75 us
  transfers between devices with their start and end apart: 4, of which 3 were waited for; matrix products, arithmetic and copies ran while one was open for 0% of the time, Pallas kernels for 0%

profile of v5, /device:TPU:0, one launch (start us, length us, event | category | flops | bytes accessed | tf_op | source)
XLA Modules:
  0.0 109.1 jit_solution(15794082730985262577)
XLA Ops:
  1.3 2.7 %shard_map.140 = f32[32,20,8,128]{3,2,1,0:T(8,128)S(1)} custom-call(s32[1]{0:T(128)S(6)} %copy.15.present_ref, f32[2,10,64,128]{3,2,1,0:T(8,128)} %bitcast.12, bf16[4,2,10,64,128]{4,3,2,1,0:T(8,128)(2,1)} %bitcast.10, bf16[256,768]{1,0:T(8,128)(2,1)} %constant.16.clone.table_hbm), custom_call_target="tpu_custom_call" | custom-call | tf_op jit(solution)/shard_map/pallas_call | solution.py:373
  4.0 0.0 copy-start.2
  4.0 0.0 copy-start.3
  4.1 0.0 copy-start.4
  4.1 0.0 copy-start.6
  4.1 0.0 copy-start.7
  4.1 0.0 copy-start.8
  4.1 0.0 copy-start.9
  4.1 0.0 copy-start.10
  4.1 42.8 %all_to_all.10.in_ref = f32[32,20,8,128]{3,2,1,0:T(8,128)S(1)} all-to-all(f32[32,20,8,128]{3,2,1,0:T(8,128)S(1)} %shard_map.140), channel_id=1, replica_groups=mesh['contrast'=4,'pa'=2,'pb'=16] {'pa','pb'}, dimensions={0} | all-to-all | bytes 5242880 | tf_op jit(solution)/shard_map/all_to_all | solution.py:386
  46.9 0.0 copy-done.2
  46.9 0.0 copy-done.3
  46.9 0.0 copy-done.4
  46.9 0.0 copy-done.6
  46.9 0.0 copy-done.7
  46.9 0.0 copy-done.8
  47.0 0.0 copy-done.9
  47.0 0.0 copy-done.10
  47.0 5.3 %shard_map.141 = f32[32,21,8,128]{3,2,1,0:T(8,128)S(1)} custom-call(s32[1]{0:T(128)S(6)} %copy.15.present_ref, f32[32,20,8,128]{3,2,1,0:T(8,128)S(1)} %all_to_all.10.in_ref, bf16[768,256]{1,0:T(8,128)(2,1)S(1)} %copy-done.4, bf16[768,256]{1,0:T(8,128)(2,1)S(1)} %copy-done.3, bf16[4,2,4,160,128]{4,3,2,1,0:T(8,128)(2,1)S(1)} %bitcast.14, ...), custom_call_target="tpu_custom_call" | custom-call | tf_op jit(solution)/shard_map/pallas_call | solution.py:387
  52.3 0.0 copy-start
  52.3 0.0 copy-start.1
  52.3 0.0 copy-start.5
  52.3 39.0 %all_to_all.11.in_ref = f32[32,21,8,128]{3,2,1,0:T(8,128)S(1)} all-to-all(f32[32,21,8,128]{3,2,1,0:T(8,128)S(1)} %shard_map.141), channel_id=1, replica_groups=mesh['contrast'=4,'pa'=2,'pb'=16] {'pa','pb'}, dimensions={0} | all-to-all | bytes 5505024 | tf_op jit(solution)/shard_map/all_to_all | solution.py:397
  91.4 0.0 copy-done
  91.4 0.0 copy-done.1
  91.4 0.0 copy-done.5
  91.4 1.5 %shard_map.142 = (f32[2,10,64,128]{3,2,1,0:T(8,128)S(1)}, f32[41,8,128]{2,1,0:T(8,128)S(1)}, f32[40,8,128]{2,1,0:T(8,128)S(1)}) custom-call(s32[1]{0:T(128)S(6)} %copy.15.present_ref, f32[32,21,8,128]{3,2,1,0:T(8,128)S(1)} %all_to_all.11.in_ref, bf16[4,2,10,64,128]{4,3,2,1,0:T(8,128)(2,1)S(1)} %bitcast.11, f32[2,10,64,128]{3,2,1,0:T(8,128)S(1)} %bitcast.13, ...), custom_call_target="tpu_custom_call" | custom-call | tf_op jit(solution)/shard_map/pallas_call | solution.py:402
  92.8 1.6 %collective-permute-start = (f32[41,8,128]{2,1,0:T(8,128)S(1)}, f32[41,8,128]{2,1,0:T(8,128)S(1)}, u32[]{:S(2)}, u32[]{:S(2)}) collective-permute-start(f32[41,8,128]{2,1,0:T(8,128)S(1)} %get-tuple-element.8), channel_id=1, source_target_pairs={{0,32},{32,0},{64,96},{96,64},{48,80},{80,48},{112,16},{16,112},{1... | collective-permute-start | bytes 503816 | tf_op jit(solution)/shard_map/ppermute | solution.py:425
  94.4 2.1 %collective-permute-start.1 = (f32[40,8,128]{2,1,0:T(8,128)S(1)}, f32[40,8,128]{2,1,0:T(8,128)S(1)}, u32[]{:S(2)}, u32[]{:S(2)}) collective-permute-start(f32[40,8,128]{2,1,0:T(8,128)S(1)} %get-tuple-element.9), channel_id=1, source_target_pairs={{32,64},{64,32},{96,0},{0,96},{16,48},{48,16},{80,112},{112,80},{3... | collective-permute-start | bytes 491528 | tf_op jit(solution)/shard_map/ppermute | solution.py:425
  96.5 2.9 %collective-permute-done = f32[41,8,128]{2,1,0:T(8,128)S(1)} collective-permute-done((f32[41,8,128]{2,1,0:T(8,128)S(1)}, f32[41,8,128]{2,1,0:T(8,128)S(1)}, u32[]{:S(2)}, u32[]{:S(2)}) %collective-permute-start) | collective-permute-done | bytes 167968 | tf_op jit(solution)/shard_map/ppermute | solution.py:425
  99.4 2.0 %collective-permute-start.2 = (f32[41,8,128]{2,1,0:T(8,128)S(1)}, f32[41,8,128]{2,1,0:T(8,128)S(1)}, u32[]{:S(2)}, u32[]{:S(2)}) collective-permute-start(f32[41,8,128]{2,1,0:T(8,128)S(1)} %add.6.refs_1_), channel_id=1, source_target_pairs={{32,64},{64,32},{96,0},{0,96},{16,48},{48,16},{80,112},{112,80},{3... | collective-permute-start | bytes 503816 | tf_op jit(solution)/shard_map/ppermute | solution.py:425
  101.4 0.0 collective-permute-done.1
  101.4 0.4 collective-permute-start.3
  101.8 5.0 %collective-permute-done.3.refs_4_ = f32[40,8,128]{2,1,0:T(8,128)S(1)} collective-permute-done((f32[40,8,128]{2,1,0:T(8,128)S(1)}, f32[40,8,128]{2,1,0:T(8,128)S(1)}, u32[]{:S(2)}, u32[]{:S(2)}) %collective-permute-start.3) | collective-permute-done | bytes 163872 | tf_op jit(solution)/shard_map/ppermute | solution.py:425
  106.8 0.8 collective-permute-done.2.refs_3_
  107.6 1.5 %shard_map.143 = (f32[2,10,64,128]{3,2,1,0:T(8,128)}, f32[1,1]{1,0:T(1,128)}) custom-call(f32[2,10,64,128]{3,2,1,0:T(8,128)S(1)} %get-tuple-element.7.refs_0_, f32[41,8,128]{2,1,0:T(8,128)S(1)} %add.6.refs_1_, f32[40,8,128]{2,1,0:T(8,128)S(1)} %add.7.refs_2_, f32[41,8,128]{2,1,0:T(8,128)S(1)} %collective-permute-done.2.refs_3_, ...), custom_call_target="tpu_custom_call" | custom-call | tf_op jit(solution)/shard_map/pallas_call | solution.py:429
  (2 shorter events, 0.0 us)
Async XLA Ops:
  4.0 42.9 %copy-start.2 = (bf16[1,4,2,4,160,128]{5,4,3,2,1,0:T(8,128)(2,1)S(1)}, bf16[1,4,2,4,160,128]{5,4,3,2,1,0:T(8,128)(2,1)}, u32[]{:S(2)}) copy-start(bf16[1,4,2,4,160,128]{5,4,3,2,1,0:T(8,128)(2,1)} %param.15) | copy-start | bytes 3932164
  4.0 42.9 %copy-start.3 = (bf16[768,256]{1,0:T(8,128)(2,1)S(1)}, bf16[768,256]{1,0:T(8,128)(2,1)}, u32[]{:S(2)}) copy-start(bf16[768,256]{1,0:T(8,128)(2,1)} %constant.19.clone.xi_ref) | copy-start | bytes 1179652
  4.1 42.9 %copy-start.4 = (bf16[768,256]{1,0:T(8,128)(2,1)S(1)}, bf16[768,256]{1,0:T(8,128)(2,1)}, u32[]{:S(2)}) copy-start(bf16[768,256]{1,0:T(8,128)(2,1)} %constant.18.clone.xf_ref) | copy-start | bytes 1179652
  4.1 42.9 %copy-start.6 = (s32[1,4,160,128]{3,2,1,0:T(8,128)S(1)}, s32[1,4,160,128]{3,2,1,0:T(8,128)}, u32[]{:S(2)}) copy-start(s32[1,4,160,128]{3,2,1,0:T(8,128)} %param.16) | copy-start | bytes 983044
  4.1 42.9 %copy-start.7 = (bf16[160,240]{1,0:T(8,128)(2,1)S(1)}, bf16[160,240]{1,0:T(8,128)(2,1)}, u32[]{:S(2)}) copy-start(bf16[160,240]{1,0:T(8,128)(2,1)} %constant.23.clone.yio_ref) | copy-start | bytes 230404
  4.1 42.9 %copy-start.8 = (bf16[160,240]{1,0:T(8,128)(2,1)S(1)}, bf16[160,240]{1,0:T(8,128)(2,1)}, u32[]{:S(2)}) copy-start(bf16[160,240]{1,0:T(8,128)(2,1)} %constant.22.clone.yfo_ref) | copy-start | bytes 230404
  4.1 42.8 %copy-start.9 = (bf16[160,240]{1,0:T(8,128)(2,1)S(1)}, bf16[160,240]{1,0:T(8,128)(2,1)}, u32[]{:S(2)}) copy-start(bf16[160,240]{1,0:T(8,128)(2,1)} %constant.21.clone.yie_ref) | copy-start | bytes 230404
  4.1 42.8 %copy-start.10 = (bf16[160,240]{1,0:T(8,128)(2,1)S(1)}, bf16[160,240]{1,0:T(8,128)(2,1)}, u32[]{:S(2)}) copy-start(bf16[160,240]{1,0:T(8,128)(2,1)} %constant.20.clone.yfe_ref) | copy-start | bytes 230404
  52.3 39.1 %copy-start = (bf16[4,2,64,10,128]{4,2,3,1,0:T(8,128)(2,1)S(1)}, bf16[4,2,64,10,128]{4,2,3,1,0:T(8,128)(2,1)}, u32[]{:S(2)}) copy-start(bf16[4,2,64,10,128]{4,2,3,1,0:T(8,128)(2,1)} %param.14) | copy-start | bytes 3932164
  52.3 39.1 %copy-start.1 = (f32[1,2,64,10,128]{4,2,3,1,0:T(8,128)S(1)}, f32[1,2,64,10,128]{4,2,3,1,0:T(8,128)}, u32[]{:S(2)}) copy-start(f32[1,2,64,10,128]{4,2,3,1,0:T(8,128)} %param.13) | copy-start | bytes 1966084
  52.3 39.1 %copy-start.5 = (bf16[768,256]{1,0:T(8,128)(2,1)S(1)}, bf16[768,256]{1,0:T(8,128)(2,1)}, u32[]{:S(2)}) copy-start(bf16[768,256]{1,0:T(8,128)(2,1)} %constant.17.clone.table_ref) | copy-start | bytes 1179652
  92.8 6.5 %collective-permute-start = (f32[41,8,128]{2,1,0:T(8,128)S(1)}, f32[41,8,128]{2,1,0:T(8,128)S(1)}, u32[]{:S(2)}, u32[]{:S(2)}) collective-permute-start(f32[41,8,128]{2,1,0:T(8,128)S(1)} %get-tuple-element.8), channel_id=1, source_target_pairs={{0,32},{32,0},{64,96},{96,64},{48,80},{80,48},{112,16},{16,112},{1... | collective-permute-start | bytes 503816 | tf_op jit(solution)/shard_map/ppermute | solution.py:425
  94.4 6.9 %collective-permute-start.1 = (f32[40,8,128]{2,1,0:T(8,128)S(1)}, f32[40,8,128]{2,1,0:T(8,128)S(1)}, u32[]{:S(2)}, u32[]{:S(2)}) collective-permute-start(f32[40,8,128]{2,1,0:T(8,128)S(1)} %get-tuple-element.9), channel_id=1, source_target_pairs={{32,64},{64,32},{96,0},{0,96},{16,48},{48,16},{80,112},{112,80},{3... | collective-permute-start | bytes 491528 | tf_op jit(solution)/shard_map/ppermute | solution.py:425
  99.4 8.2 %collective-permute-start.2 = (f32[41,8,128]{2,1,0:T(8,128)S(1)}, f32[41,8,128]{2,1,0:T(8,128)S(1)}, u32[]{:S(2)}, u32[]{:S(2)}) collective-permute-start(f32[41,8,128]{2,1,0:T(8,128)S(1)} %add.6.refs_1_), channel_id=1, source_target_pairs={{32,64},{64,32},{96,0},{0,96},{16,48},{48,16},{80,112},{112,80},{3... | collective-permute-start | bytes 503816 | tf_op jit(solution)/shard_map/ppermute | solution.py:425
  101.4 5.4 %collective-permute-start.3 = (f32[40,8,128]{2,1,0:T(8,128)S(1)}, f32[40,8,128]{2,1,0:T(8,128)S(1)}, u32[]{:S(2)}, u32[]{:S(2)}) collective-permute-start(f32[40,8,128]{2,1,0:T(8,128)S(1)} %add.7.refs_2_), channel_id=1, source_target_pairs={{0,32},{32,0},{64,96},{96,64},{48,80},{80,48},{112,16},{16,112},{1... | collective-permute-start | bytes 491528 | tf_op jit(solution)/shard_map/ppermute | solution.py:425

commit v6 on v5

--- a/solution.py
+++ b/solution.py
@@ -13,7 +13,6 @@
 step_size = 1.0
 threshold = 2.5
 LANES = 128
-CHUNKS = 2
 VMEM_LIMIT = 40 * 1024 * 1024
 
 
@@ -275,63 +274,70 @@
 
 
 def z_inverse_kernel(
-    scale, present_ref, in_ref, maps_ref, image_ref, table_ref, moved_ref, *energy_refs
+    scale, first, present_ref, in_ref, maps_ref, image_ref, table_ref, moved_ref, energy_ref
 ):
-    parts, _, sub, _ = in_ref.shape
+    parts, stored, sub, _ = in_ref.shape
     coils = maps_ref.shape[0]
-    _, y_rows, x_rows, depth = image_ref.shape
+    _, y_rows, x_rows, depth = moved_ref.shape
     rows = y_rows * x_rows
-    tiles = rows // LANES
+    tiles = (stored - 1) // coils
+    along = pl.ds(first * LANES // x_rows, y_rows)
+    present = present_ref[0].astype(jnp.float32)
     grad_re = jnp.zeros((rows, depth), jnp.float32)
     grad_im = jnp.zeros((rows, depth), jnp.float32)
     for coil in range(coils):
         data = jnp.concatenate(
-            [in_ref[:, coil * tiles + t].reshape(parts * sub, LANES) for t in range(tiles)], axis=1
+            [
+                in_ref[:, coil * tiles + first + t].reshape(parts * sub, LANES)
+                for t in range(rows // LANES)
+            ],
+            axis=1,
         )
         result = dot(split_data(data, 0), table_ref[...], ((0,), (0,)))
         back_re = result[:, :depth]
         back_im = result[:, depth:]
-        maps_re = maps_ref[coil, 0].reshape(rows, depth).astype(jnp.float32)
-        maps_im = maps_ref[coil, 1].reshape(rows, depth).astype(jnp.float32)
+        maps_re = maps_ref[coil, 0, along].reshape(rows, depth).astype(jnp.float32)
+        maps_im = maps_ref[coil, 1, along].reshape(rows, depth).astype(jnp.float32)
         grad_re = grad_re + (maps_re * back_re + maps_im * back_im)
         grad_im = grad_im + (maps_re * back_im - maps_im * back_re)
-    shape = image_ref.shape[1:]
-    moved_re = image_ref[0] - step_size * grad_re.reshape(shape)
-    moved_im = image_ref[1] - step_size * grad_im.reshape(shape)
-    present = present_ref[0].astype(jnp.float32)
+    shape = moved_ref.shape[1:]
+    moved_re = image_ref[0, along] - step_size * grad_re.reshape(shape)
+    moved_im = image_ref[1, along] - step_size * grad_im.reshape(shape)
     moved_ref[0] = present * moved_re
     moved_ref[1] = present * moved_im
     energy = present * (moved_re * moved_re + moved_im * moved_im)
-    energy = energy.reshape(rows // 8, 8, depth)
-    cut = rows // 8 // len(energy_refs)
-    for n, energy_ref in enumerate(energy_refs):
-        energy_ref[:cut] = energy[n * cut : (n + 1) * cut]
-    misfit = jnp.sum(in_ref[:, coils * tiles], axis=0)
-    energy_refs[0][cut] = jnp.full((8, depth), jnp.sum(misfit) * scale)
-
-
-def shrink_kernel(*refs):
-    moved_ref = refs[0]
-    energy_refs, other_refs = refs[1 : 1 + CHUNKS], refs[1 + CHUNKS : 1 + 2 * CHUNKS]
-    image_hbm, misfit_ref, image_ref, sems = refs[1 + 2 * CHUNKS :]
-    parts, y_rows, x_rows, depth = moved_ref.shape
-    cut = y_rows // CHUNKS
-    count = cut * x_rows // 8
-    copies = []
-    for n in range(CHUNKS):
-        rows = pl.ds(n * cut, cut)
-        energy = energy_refs[n][:count] + other_refs[n][:count]
-        norm_value = jnp.sqrt(energy.reshape(cut, x_rows, depth))
-        factor = jnp.maximum(norm_value - threshold, 0.0) / jnp.maximum(norm_value, threshold)
-        for part in range(parts):
-            image_ref[part, rows] = moved_ref[part, rows] * factor
-        copies.append(
-            pltpu.make_async_copy(image_ref.at[:, rows], image_hbm.at[:, rows], sems.at[n])
-        )
-        copies[-1].start()
-    misfit_ref[0, 0] = jnp.max(energy_refs[0][count] + other_refs[0][count])
-    for copy in copies:
-        copy.wait()
+    energy_ref[: rows // 8] = energy.reshape(rows // 8, 8, depth)
+    if first == 0:
+        misfit = jnp.sum(in_ref[:, coils * tiles], axis=0)
+        energy_ref[rows // 8] = jnp.full((8, depth), jnp.sum(misfit) * scale)
+
+
+def shrunk(moved_ref, energy_ref, other_ref, image_ref):
+    shape = moved_ref.shape[1:]
+    count = shape[0] * shape[1] // 8
+    norm_value = jnp.sqrt((energy_ref[:count] + other_ref[:count]).reshape(shape))
+    factor = jnp.maximum(norm_value - threshold, 0.0) / jnp.maximum(norm_value, threshold)
+    for part in range(2):
+        image_ref[part] = moved_ref[part] * factor
+    return count
+
+
+def shrink_first_kernel(moved_ref, energy_ref, other_ref, image_hbm, misfit_ref, image_ref, sem):
+    count = shrunk(moved_ref, energy_ref, other_ref, image_ref)
+    copy = pltpu.make_async_copy(image_ref, image_hbm.at[:, pl.ds(0, moved_ref.shape[1])], sem)
+    copy.start()
+    misfit_ref[0, 0] = jnp.max(energy_ref[count] + other_ref[count])
+    copy.wait()
+
+
+def shrink_rest_kernel(moved_ref, energy_ref, other_ref, _, image_hbm, image_ref, sem):
+    shrunk(moved_ref, energy_ref, other_ref, image_ref)
+    rows = moved_ref.shape[1]
+    copy = pltpu.make_async_copy(
+        image_ref, image_hbm.at[:, pl.ds(image_hbm.shape[1] - rows, rows)], sem
+    )
+    copy.start()
+    copy.wait()
 
 
 def params():
@@ -398,20 +404,21 @@
 
     contrasts = lax.axis_size("contrast") * image.shape[0]
     scale = 1.0 / (2.0 * contrasts * coils * width_x * width_y * depth)
-    energy_tiles = y_rows * x_rows // 8 // CHUNKS
-    moved, *energies = pl.pallas_call(
-        functools.partial(z_inverse_kernel, scale),
-        out_shape=(
-            jax.ShapeDtypeStruct(pixels.shape, jnp.float32),
-            *[
-                jax.ShapeDtypeStruct((energy_tiles + (n == 0), 8, depth), jnp.float32)
-                for n in range(CHUNKS)
-            ],
-        ),
-        in_specs=[scalar] + [local] * 4,
-        out_specs=(local,) * (1 + CHUNKS),
-        compiler_params=params(),
-    )(available, returned, maps, pixels, zi)
+    moved, energies = [], []
+    for first, last in ((0, (tiles + 1) // 2), ((tiles + 1) // 2, tiles)):
+        y_part = (last - first) * LANES // x_rows
+        moved_part, energy_part = pl.pallas_call(
+            functools.partial(z_inverse_kernel, scale, first),
+            out_shape=(
+                jax.ShapeDtypeStruct((2, y_part, x_rows, depth), jnp.float32),
+                jax.ShapeDtypeStruct((y_part * x_rows // 8 + (first == 0), 8, depth), jnp.float32),
+            ),
+            in_specs=[scalar] + [local] * 4,
+            out_specs=(local, local),
+            compiler_params=params(),
+        )(available, returned, maps, pixels, zi)
+        moved.append(moved_part)
+        energies.append(energy_part)
 
     size = lax.axis_size("contrast")
 
@@ -426,20 +433,25 @@
 
     energies = [value + other_sum(value, n) for n, value in enumerate(energies)]
     others = [other_sum(value, n + 1) for n, value in enumerate(energies)]
+    image_type = jax.ShapeDtypeStruct(pixels.shape, jnp.float32)
+    scratch = [[pltpu.VMEM(part.shape, jnp.float32), pltpu.SemaphoreType.DMA] for part in moved]
     result, misfit = pl.pallas_call(
-        shrink_kernel,
-        out_shape=(
-            jax.ShapeDtypeStruct(pixels.shape, jnp.float32),
-            jax.ShapeDtypeStruct((1, 1), jnp.float32),
-        ),
-        in_specs=[local] * (1 + 2 * CHUNKS),
+        shrink_first_kernel,
+        out_shape=(image_type, jax.ShapeDtypeStruct((1, 1), jnp.float32)),
+        in_specs=[local] * 3,
         out_specs=(anywhere, scalar),
-        scratch_shapes=[
-            pltpu.VMEM(pixels.shape, jnp.float32),
-            pltpu.SemaphoreType.DMA((CHUNKS,)),
-        ],
+        scratch_shapes=scratch[0],
         compiler_params=params(),
-    )(moved, *energies, *others)
+    )(moved[0], energies[0], others[0])
+    result = pl.pallas_call(
+        shrink_rest_kernel,
+        out_shape=image_type,
+        in_specs=[local] * 3 + [anywhere],
+        out_specs=anywhere,
+        scratch_shapes=scratch[1],
+        input_output_aliases={3: 0},
+        compiler_params=params(),
+    )(moved[1], energies[1], others[1], result)
     return (jnp.transpose(result, (0, 2, 1, 3))[None], misfit[0, 0])
 
 

time: 110 us -> 110 us (level)
  waiting for transfers between devices: 8.72 us -> 7.08 us
    ppermute x4, waiting for transfers between devices: 8.72 us -> 7.08 us  [other_sum(): return lax.ppermute(value, ('contrast', 'pa'), pairs)]
    pallas_call x2 -> x4, Pallas kernels: 2.93 us -> 3.93 us  [the longest x2 1.73 us: per_device(): pl.pallas_call(functools.partial(z_inverse_kernel, scale, first), out_sha...]
  transfers between devices with their start and end apart: 4 -> 4, of which waited for: 3 -> 2; matrix products, arithmetic and copies ran while one was open for 0% -> 0% of each run, Pallas kernels for 0% -> 2%
where the time goes in v6:
time: 110 us; the launch traced here: 109 us
  blocking collectives  81.8 us (74%)
  Pallas kernels  12 us (11%)
  waiting for transfers between devices  7.08 us (6%)
  starting transfers between devices  6.94 us (6%)
  between operations  1.47 us (1%)
    all_to_all x1, blocking collectives, per_device(): lax.all_to_all(forward, ('pa', 'pb'), split_axis=0, concat_axis=0, tiled=...  42.8 us
    all_to_all x1, blocking collectives, per_device(): lax.all_to_all(residual, ('pa', 'pb'), split_axis=0, concat_axis=0, tiled...  39 us
    ppermute x4, waiting for transfers between devices, other_sum(): return lax.ppermute(value, ('contrast', 'pa'), pairs)  7.08 us
    ppermute x4, starting transfers between devices, other_sum(): return lax.ppermute(value, ('contrast', 'pa'), pairs)  6.94 us
    pallas_call x1, Pallas kernels, per_device(): pl.pallas_call(functools.partial(plane_kernel, 1), out_shape=jax.ShapeDty...  5.32 us
    pallas_call x1, Pallas kernels, per_device(): pl.pallas_call(functools.partial(z_forward_kernel, 1), out_shape=jax.Shap...  2.75 us
  transfers between devices with their start and end apart: 4, of which 2 were waited for; matrix products, arithmetic and copies ran while one was open for 0% of the time, Pallas kernels for 2%

profile of v6, /device:TPU:0, one launch (start us, length us, event | category | flops | bytes accessed | tf_op | source)
XLA Modules:
  0.0 109.4 jit_solution(193097551136428160)
XLA Ops:
  1.3 2.7 %shard_map.140 = f32[32,20,8,128]{3,2,1,0:T(8,128)S(1)} custom-call(s32[1]{0:T(128)S(6)} %copy.17.present_ref, f32[2,10,64,128]{3,2,1,0:T(8,128)} %bitcast.13, bf16[4,2,10,64,128]{4,3,2,1,0:T(8,128)(2,1)} %bitcast.10, bf16[256,768]{1,0:T(8,128)(2,1)} %constant.16.clone.table_hbm), custom_call_target="tpu_custom_call" | custom-call | tf_op jit(solution)/shard_map/pallas_call | solution.py:379
  4.0 0.0 copy-start.3
  4.0 0.0 copy-start.4
  4.1 0.0 copy-start.5
  4.1 0.0 copy-start.6
  4.1 0.0 copy-start.7
  4.1 0.0 copy-start.8
  4.1 0.0 copy-start.9
  4.1 0.0 copy-start.10
  4.1 42.8 %all_to_all.10.in_ref = f32[32,20,8,128]{3,2,1,0:T(8,128)S(1)} all-to-all(f32[32,20,8,128]{3,2,1,0:T(8,128)S(1)} %shard_map.140), channel_id=1, replica_groups=mesh['contrast'=4,'pa'=2,'pb'=16] {'pa','pb'}, dimensions={0} | all-to-all | bytes 5242880 | tf_op jit(solution)/shard_map/all_to_all | solution.py:392
  46.9 0.0 copy-done.3
  46.9 0.0 copy-done.4
  46.9 0.0 copy-done.5
  46.9 0.0 copy-done.6
  46.9 0.0 copy-done.7
  46.9 0.0 copy-done.8
  47.0 0.0 copy-done.9
  47.0 0.0 copy-done.10
  47.0 5.3 %shard_map.141 = f32[32,21,8,128]{3,2,1,0:T(8,128)S(1)} custom-call(s32[1]{0:T(128)S(6)} %copy.17.present_ref, f32[32,20,8,128]{3,2,1,0:T(8,128)S(1)} %all_to_all.10.in_ref, bf16[768,256]{1,0:T(8,128)(2,1)S(1)} %copy-done.5, bf16[768,256]{1,0:T(8,128)(2,1)S(1)} %copy-done.4, bf16[4,2,4,160,128]{4,3,2,1,0:T(8,128)(2,1)S(1)} %bitcast.16, ...), custom_call_target="tpu_custom_call" | custom-call | tf_op jit(solution)/shard_map/pallas_call | solution.py:393
  52.3 0.0 copy-start
  52.3 0.0 copy-start.1
  52.3 0.0 copy-start.2
  52.3 39.0 %all_to_all.11.in_ref = f32[32,21,8,128]{3,2,1,0:T(8,128)S(1)} all-to-all(f32[32,21,8,128]{3,2,1,0:T(8,128)S(1)} %shard_map.141), channel_id=1, replica_groups=mesh['contrast'=4,'pa'=2,'pb'=16] {'pa','pb'}, dimensions={0} | all-to-all | bytes 5505024 | tf_op jit(solution)/shard_map/all_to_all | solution.py:403
  91.4 0.0 copy-done
  91.4 0.0 copy-done.1
  91.4 0.0 copy-done.2
  91.4 1.0 shard_map.143
  92.4 1.6 %collective-permute-start.2 = (f32[49,8,128]{2,1,0:T(8,128)S(1)}, f32[49,8,128]{2,1,0:T(8,128)S(1)}, u32[]{:S(2)}, u32[]{:S(2)}) collective-permute-start(f32[49,8,128]{2,1,0:T(8,128)S(1)} %get-tuple-element.11), channel_id=1, source_target_pairs={{0,32},{32,0},{64,96},{96,64},{48,80},{80,48},{112,16},{16,112},{1... | collective-permute-start | bytes 602120 | tf_op jit(solution)/shard_map/ppermute | solution.py:432
  94.0 0.7 shard_map.142
  94.7 2.2 %collective-permute-start = (f32[32,8,128]{2,1,0:T(8,128)S(1)}, f32[32,8,128]{2,1,0:T(8,128)S(1)}, u32[]{:S(2)}, u32[]{:S(2)}) collective-permute-start(f32[32,8,128]{2,1,0:T(8,128)S(1)} %get-tuple-element.9), channel_id=1, source_target_pairs={{32,64},{64,32},{96,0},{0,96},{16,48},{48,16},{80,112},{112,80},{3... | collective-permute-start | bytes 393224 | tf_op jit(solution)/shard_map/ppermute | solution.py:432
  96.9 2.0 %collective-permute-done.2 = f32[49,8,128]{2,1,0:T(8,128)S(1)} collective-permute-done((f32[49,8,128]{2,1,0:T(8,128)S(1)}, f32[49,8,128]{2,1,0:T(8,128)S(1)}, u32[]{:S(2)}, u32[]{:S(2)}) %collective-permute-start.2) | collective-permute-done | bytes 200736 | tf_op jit(solution)/shard_map/ppermute | solution.py:432
  98.9 2.8 %collective-permute-start.3 = (f32[49,8,128]{2,1,0:T(8,128)S(1)}, f32[49,8,128]{2,1,0:T(8,128)S(1)}, u32[]{:S(2)}, u32[]{:S(2)}) collective-permute-start(f32[49,8,128]{2,1,0:T(8,128)S(1)} %add.7.energy_ref), channel_id=1, source_target_pairs={{32,64},{64,32},{96,0},{0,96},{16,48},{48,16},{80,112},{112,80},{3... | collective-permute-start | bytes 602120 | tf_op jit(solution)/shard_map/ppermute | solution.py:432
  101.7 0.0 collective-permute-done
  101.8 0.4 collective-permute-start.1
  102.1 5.1 %collective-permute-done.3.other_ref = f32[49,8,128]{2,1,0:T(8,128)S(1)} collective-permute-done((f32[49,8,128]{2,1,0:T(8,128)S(1)}, f32[49,8,128]{2,1,0:T(8,128)S(1)}, u32[]{:S(2)}, u32[]{:S(2)}) %collective-permute-start.3) | collective-permute-done | bytes 200736 | tf_op jit(solution)/shard_map/ppermute | solution.py:432
  107.2 1.4 %shard_map.144 = (f32[2,10,64,128]{3,2,1,0:T(8,128)}, f32[1,1]{1,0:T(1,128)}) custom-call(f32[2,6,64,128]{3,2,1,0:T(8,128)S(1)} %get-tuple-element.10.moved_ref, f32[49,8,128]{2,1,0:T(8,128)S(1)} %add.7.energy_ref, f32[49,8,128]{2,1,0:T(8,128)S(1)} %collective-permute-done.3.other_ref), custom_call_target="tpu_custom_call" | custom-call | tf_op jit(solution)/shard_map/pallas_call | solution.py:438
  108.6 0.0 collective-permute-done.1.other_ref
  108.6 0.8 shard_map.145
  (2 shorter events, 0.0 us)
Async XLA Ops:
  4.0 42.9 %copy-start.3 = (bf16[1,4,2,4,160,128]{5,4,3,2,1,0:T(8,128)(2,1)S(1)}, bf16[1,4,2,4,160,128]{5,4,3,2,1,0:T(8,128)(2,1)}, u32[]{:S(2)}) copy-start(bf16[1,4,2,4,160,128]{5,4,3,2,1,0:T(8,128)(2,1)} %param.15) | copy-start | bytes 3932164
  4.0 42.9 %copy-start.4 = (bf16[768,256]{1,0:T(8,128)(2,1)S(1)}, bf16[768,256]{1,0:T(8,128)(2,1)}, u32[]{:S(2)}) copy-start(bf16[768,256]{1,0:T(8,128)(2,1)} %constant.19.clone.xi_ref) | copy-start | bytes 1179652
  4.1 42.9 %copy-start.5 = (bf16[768,256]{1,0:T(8,128)(2,1)S(1)}, bf16[768,256]{1,0:T(8,128)(2,1)}, u32[]{:S(2)}) copy-start(bf16[768,256]{1,0:T(8,128)(2,1)} %constant.18.clone.xf_ref) | copy-start | bytes 1179652
  4.1 42.9 %copy-start.6 = (s32[1,4,160,128]{3,2,1,0:T(8,128)S(1)}, s32[1,4,160,128]{3,2,1,0:T(8,128)}, u32[]{:S(2)}) copy-start(s32[1,4,160,128]{3,2,1,0:T(8,128)} %param.16) | copy-start | bytes 983044
  4.1 42.9 %copy-start.7 = (bf16[160,240]{1,0:T(8,128)(2,1)S(1)}, bf16[160,240]{1,0:T(8,128)(2,1)}, u32[]{:S(2)}) copy-start(bf16[160,240]{1,0:T(8,128)(2,1)} %constant.23.clone.yio_ref) | copy-start | bytes 230404
  4.1 42.9 %copy-start.8 = (bf16[160,240]{1,0:T(8,128)(2,1)S(1)}, bf16[160,240]{1,0:T(8,128)(2,1)}, u32[]{:S(2)}) copy-start(bf16[160,240]{1,0:T(8,128)(2,1)} %constant.22.clone.yfo_ref) | copy-start | bytes 230404
  4.1 42.8 %copy-start.9 = (bf16[160,240]{1,0:T(8,128)(2,1)S(1)}, bf16[160,240]{1,0:T(8,128)(2,1)}, u32[]{:S(2)}) copy-start(bf16[160,240]{1,0:T(8,128)(2,1)} %constant.21.clone.yie_ref) | copy-start | bytes 230404
  4.1 42.8 %copy-start.10 = (bf16[160,240]{1,0:T(8,128)(2,1)S(1)}, bf16[160,240]{1,0:T(8,128)(2,1)}, u32[]{:S(2)}) copy-start(bf16[160,240]{1,0:T(8,128)(2,1)} %constant.20.clone.yfe_ref) | copy-start | bytes 230404
  52.3 39.1 %copy-start = (bf16[4,2,64,10,128]{4,2,3,1,0:T(8,128)(2,1)S(1)}, bf16[4,2,64,10,128]{4,2,3,1,0:T(8,128)(2,1)}, u32[]{:S(2)}) copy-start(bf16[4,2,64,10,128]{4,2,3,1,0:T(8,128)(2,1)} %param.14) | copy-start | bytes 3932164
  52.3 39.1 %copy-start.1 = (f32[1,2,64,10,128]{4,2,3,1,0:T(8,128)S(1)}, f32[1,2,64,10,128]{4,2,3,1,0:T(8,128)}, u32[]{:S(2)}) copy-start(f32[1,2,64,10,128]{4,2,3,1,0:T(8,128)} %param.13) | copy-start | bytes 1966084
  52.3 39.1 %copy-start.2 = (bf16[768,256]{1,0:T(8,128)(2,1)S(1)}, bf16[768,256]{1,0:T(8,128)(2,1)}, u32[]{:S(2)}) copy-start(bf16[768,256]{1,0:T(8,128)(2,1)} %constant.17.clone.table_ref) | copy-start | bytes 1179652
  92.4 6.5 %collective-permute-start.2 = (f32[49,8,128]{2,1,0:T(8,128)S(1)}, f32[49,8,128]{2,1,0:T(8,128)S(1)}, u32[]{:S(2)}, u32[]{:S(2)}) collective-permute-start(f32[49,8,128]{2,1,0:T(8,128)S(1)} %get-tuple-element.11), channel_id=1, source_target_pairs={{0,32},{32,0},{64,96},{96,64},{48,80},{80,48},{112,16},{16,112},{1... | collective-permute-start | bytes 602120 | tf_op jit(solution)/shard_map/ppermute | solution.py:432
  94.7 7.0 %collective-permute-start = (f32[32,8,128]{2,1,0:T(8,128)S(1)}, f32[32,8,128]{2,1,0:T(8,128)S(1)}, u32[]{:S(2)}, u32[]{:S(2)}) collective-permute-start(f32[32,8,128]{2,1,0:T(8,128)S(1)} %get-tuple-element.9), channel_id=1, source_target_pairs={{32,64},{64,32},{96,0},{0,96},{16,48},{48,16},{80,112},{112,80},{3... | collective-permute-start | bytes 393224 | tf_op jit(solution)/shard_map/ppermute | solution.py:432
  98.9 8.3 %collective-permute-start.3 = (f32[49,8,128]{2,1,0:T(8,128)S(1)}, f32[49,8,128]{2,1,0:T(8,128)S(1)}, u32[]{:S(2)}, u32[]{:S(2)}) collective-permute-start(f32[49,8,128]{2,1,0:T(8,128)S(1)} %add.7.energy_ref), channel_id=1, source_target_pairs={{32,64},{64,32},{96,0},{0,96},{16,48},{48,16},{80,112},{112,80},{3... | collective-permute-start | bytes 602120 | tf_op jit(solution)/shard_map/ppermute | solution.py:432
  101.8 6.9 %collective-permute-start.1 = (f32[32,8,128]{2,1,0:T(8,128)S(1)}, f32[32,8,128]{2,1,0:T(8,128)S(1)}, u32[]{:S(2)}, u32[]{:S(2)}) collective-permute-start(f32[32,8,128]{2,1,0:T(8,128)S(1)} %add.6.energy_ref), channel_id=1, source_target_pairs={{0,32},{32,0},{64,96},{96,64},{48,80},{80,48},{112,16},{16,112},{1... | collective-permute-start | bytes 393224 | tf_op jit(solution)/shard_map/ppermute | solution.py:432
